TPU v7x, 32 devices: a whole 2x2x4 slice. The times are simulated.
32 devices in a mesh: dp: 8 (over z, y), mp: 4 (over x, core).
Axes of the slice: x: 2, y: 2, z: 4, core: 2. Of those that a mesh axis runs over, the one named last changes fastest.
Arguments:
- inputs: bfloat16 [7840, 768], P('dp'), may hold values from -6 to 6
- image_of_row: int32 [7840], P('dp'), may hold values from 0 to 4, as said below
- gain_first: bfloat16 [768], replicated, may hold values from 0.5 to 1.5
- shift_first: bfloat16 [768], replicated, may hold values from -3 to 3
- qkv_weight: bfloat16 [3, 768, 768], P(None, None, 'mp'), may hold values from -0.21875 to 0.21875
- qv_bias: bfloat16 [2, 768], P(None, 'mp'), may hold values from -3 to 3
- out_weight: bfloat16 [768, 768], P('mp'), may hold values from -1.75 to 1.75
- out_bias: bfloat16 [768], replicated, may hold values from -3 to 3
- gain_second: bfloat16 [768], replicated, may hold values from 0.5 to 1.5
- shift_second: bfloat16 [768], replicated, may hold values from -3 to 3
- up_weight: bfloat16 [768, 3072], P(None, 'mp'), may hold values from -0.21875 to 0.21875
- up_bias: bfloat16 [3072], P('mp'), may hold values from -3 to 3
- down_weight: bfloat16 [3072, 768], P('mp'), may hold values from -0.15625 to 0.15625
- down_bias: bfloat16 [768], replicated, may hold values from -3 to 3
- cotangent: bfloat16 [7840, 768], P(('dp', 'mp')), may hold values from -6 to 6
Outputs:
- block_out: float32 [7840, 768], P(('dp', 'mp'))
- input_grad: float32 [7840, 768], P(('dp', 'mp'))
- grad_gain_first: float32 [768], replicated
- grad_shift_first: float32 [768], replicated
- grad_qkv: float32 [3, 768, 768], P(None, None, 'mp')
- grad_qv: float32 [2, 768], P(None, 'mp')
- grad_out: float32 [768, 768], P('mp')
- grad_out_bias: float32 [768], replicated
- grad_gain_second: float32 [768], replicated
- grad_shift_second: float32 [768], replicated
- grad_up: float32 [768, 3072], P(None, 'mp')
- grad_up_bias: float32 [3072], P('mp')
- grad_down: float32 [3072, 768], P('mp')
- grad_down_bias: float32 [768], replicated
Inputs may be any that keep to these rules, and one draw needn't show every extreme that they name: `image_of_row`: each index of dp holds 980 patches as 1 group of 980 rows in order; a group is either one image of 784 patches followed by one of 196, or five images of 196. Entries number the images of an index of dp from 0 upward in row order. In every draw some index of dp holds only five-image groups and some only two-image groups.
All inputs are finite; a program needn't handle non-finite values.
Results may differ from a plain program's by a relative error of at most 0.018.
Values may be sent and summed in bfloat16 or wider, within the bound.
A program may use at most 128 MiB of HBM per device.

v0:
```python
import jax
import jax.numpy as jnp
from jax import lax
from jax.sharding import PartitionSpec as P

HD = 64
P_LO = 196


EPSILON = 1e-06


def layer_hat(values):
    center = values - jnp.mean(values, axis=1, keepdims=True)
    factor = lax.rsqrt(jnp.mean(center * center, axis=1, keepdims=True) + EPSILON)
    return (center * factor, factor)


def layer_back(grad_hat, normed, factor):
    first = jnp.mean(grad_hat, axis=1, keepdims=True)
    second = jnp.mean(grad_hat * normed, axis=1, keepdims=True)
    return factor * (grad_hat - first - normed * second)


def image_forward(queries, keys_in, values_in):
    factor = queries.shape[-1] ** (-0.5)
    scores = (
        jnp.einsum("blhe,bmhe->bhlm", queries, keys_in, preferred_element_type=jnp.float32) * factor
    )
    highest = jnp.max(scores, axis=-1, keepdims=True)
    log_total = highest + jnp.log(jnp.sum(jnp.exp(scores - highest), axis=-1, keepdims=True))
    probs = jnp.exp(scores - log_total).astype(jnp.bfloat16)
    context = jnp.einsum("bhlm,bmhe->blhe", probs, values_in, preferred_element_type=jnp.float32)
    return (context.astype(jnp.bfloat16), log_total[..., 0])


def image_backward(queries, keys_in, values_in, log_total, grad_context):
    factor = queries.shape[-1] ** (-0.5)
    scores = (
        jnp.einsum("blhe,bmhe->bhlm", queries, keys_in, preferred_element_type=jnp.float32) * factor
    )
    probs = jnp.exp(scores - log_total[..., None])
    grad_values = jnp.einsum(
        "bhlm,blhe->bmhe",
        probs.astype(jnp.bfloat16),
        grad_context,
        preferred_element_type=jnp.float32,
    ).astype(jnp.bfloat16)
    grad_probs = jnp.einsum(
        "blhe,bmhe->bhlm", grad_context, values_in, preferred_element_type=jnp.float32
    )
    inner = jnp.sum(probs * grad_probs, axis=-1, keepdims=True)
    grad_scores = (probs * (grad_probs - inner)).astype(jnp.bfloat16)
    grad_queries = (
        jnp.einsum("bhlm,bmhe->blhe", grad_scores, keys_in, preferred_element_type=jnp.float32)
        * factor
    ).astype(jnp.bfloat16)
    grad_keys = (
        jnp.einsum("bhlm,blhe->bmhe", grad_scores, queries, preferred_element_type=jnp.float32)
        * factor
    ).astype(jnp.bfloat16)
    return (grad_queries, grad_keys, grad_values)


def split_two(tensor):
    return (tensor[None, : 4 * P_LO], tensor[None, 4 * P_LO :])


def split_five(tensor):
    return tensor.reshape((5, P_LO) + tensor.shape[1:])


def forward_two(group_q, group_k, group_v):
    big_q, small_q = split_two(group_q)
    big_k, small_k = split_two(group_k)
    big_v, small_v = split_two(group_v)
    big_ctx, big_total = image_forward(big_q, big_k, big_v)
    small_ctx, small_total = image_forward(small_q, small_k, small_v)
    return (
        jnp.concatenate([big_ctx[0], small_ctx[0]], axis=0),
        jnp.concatenate([big_total[0], small_total[0]], axis=1),
    )


def forward_five(group_q, group_k, group_v):
    context, log_total = image_forward(
        split_five(group_q), split_five(group_k), split_five(group_v)
    )
    heads_here = log_total.shape[1]
    return (
        context.reshape(group_q.shape),
        jnp.transpose(log_total, (1, 0, 2)).reshape(heads_here, 5 * P_LO),
    )


def backward_two(group_q, group_k, group_v, log_total, grad_context):
    big_q, small_q = split_two(group_q)
    big_k, small_k = split_two(group_k)
    big_v, small_v = split_two(group_v)
    big_g, small_g = split_two(grad_context)
    big_grads = image_backward(big_q, big_k, big_v, log_total[None, :, : 4 * P_LO], big_g)
    small_grads = image_backward(small_q, small_k, small_v, log_total[None, :, 4 * P_LO :], small_g)
    return tuple(
        (
            jnp.concatenate([big_item[0], small_item[0]], axis=0)
            for big_item, small_item in zip(big_grads, small_grads)
        )
    )


def backward_five(group_q, group_k, group_v, log_total, grad_context):
    heads_here = log_total.shape[0]
    totals = jnp.transpose(log_total.reshape(heads_here, 5, P_LO), (1, 0, 2))
    grads = image_backward(
        split_five(group_q),
        split_five(group_k),
        split_five(group_v),
        totals,
        split_five(grad_context),
    )
    return tuple((item.reshape(group_q.shape) for item in grads))


def per_device(
    inputs,
    image_of_row,
    gain_first,
    shift_first,
    qkv_weight,
    qv_bias,
    out_weight,
    out_bias,
    gain_second,
    shift_second,
    up_weight,
    up_bias,
    down_weight,
    down_bias,
    cotangent,
):
    rows = inputs.shape[0]
    local_width = qkv_weight.shape[2]
    heads_here = local_width // HD
    share = rows // lax.axis_size("mp")
    offset = lax.axis_index("mp") * share
    groups = rows // (5 * P_LO)
    gain_a = gain_first.astype(jnp.float32)
    shift_a = shift_first.astype(jnp.float32)
    gain_b = gain_second.astype(jnp.float32)
    shift_b = shift_second.astype(jnp.float32)
    wide_in = inputs.astype(jnp.float32)
    normed_first, factor_first = layer_hat(wide_in)
    act_first = (normed_first * gain_a + shift_a).astype(jnp.bfloat16)
    projected = jnp.einsum("rd,cde->cre", act_first, qkv_weight, preferred_element_type=jnp.float32)
    bias_wide = qv_bias.astype(jnp.float32)
    queries = (
        (projected[0] + bias_wide[0]).astype(jnp.bfloat16).reshape(groups, 5 * P_LO, heads_here, HD)
    )
    keys_all = projected[1].astype(jnp.bfloat16).reshape(groups, 5 * P_LO, heads_here, HD)
    values_all = (
        (projected[2] + bias_wide[1]).astype(jnp.bfloat16).reshape(groups, 5 * P_LO, heads_here, HD)
    )
    group_ids = image_of_row.reshape(groups, 5 * P_LO)
    single_big = group_ids[:, 0] == group_ids[:, 4 * P_LO - 1]

    def forward_group(packed):
        flag, group_q, group_k, group_v = packed
        return lax.cond(flag, forward_two, forward_five, group_q, group_k, group_v)

    context, log_totals = lax.map(forward_group, (single_big, queries, keys_all, values_all))
    context = context.reshape(rows, local_width)
    bias_out = out_bias.astype(jnp.float32)
    attn_total = lax.psum(
        jnp.dot(context, out_weight, preferred_element_type=jnp.float32).astype(jnp.bfloat16), "mp"
    ).astype(jnp.float32)
    resid_all = wide_in + attn_total + bias_out
    normed_all, factor_all = layer_hat(resid_all)
    act_second = (normed_all * gain_b + shift_b).astype(jnp.bfloat16)
    resid_share = lax.dynamic_slice_in_dim(resid_all, offset, share, 0)
    normed_two = lax.dynamic_slice_in_dim(normed_all, offset, share, 0)
    factor_two = lax.dynamic_slice_in_dim(factor_all, offset, share, 0)
    hidden_pre = jnp.dot(
        act_second, up_weight, preferred_element_type=jnp.float32
    ) + up_bias.astype(jnp.float32)
    hidden = jax.nn.gelu(hidden_pre, approximate=False).astype(jnp.bfloat16)
    mlp_part = lax.psum_scatter(
        jnp.dot(hidden, down_weight, preferred_element_type=jnp.float32).astype(jnp.bfloat16),
        "mp",
        scatter_dimension=0,
        tiled=True,
    ).astype(jnp.float32)
    block_out = resid_share + mlp_part + down_bias.astype(jnp.float32)
    contract_rows = (((0,), (0,)), ((), ()))
    contract_cols = (((1,), (1,)), ((), ()))
    cot_all = lax.all_gather(cotangent, "mp", axis=0, tiled=True)
    grad_down = lax.dot_general(hidden, cot_all, contract_rows, preferred_element_type=jnp.float32)
    grad_hidden = lax.dot_general(
        cot_all, down_weight, contract_cols, preferred_element_type=jnp.float32
    )
    gelu_pull = jax.vjp(lambda preact: jax.nn.gelu(preact, approximate=False), hidden_pre)[1]
    grad_pre = gelu_pull(grad_hidden)[0].astype(jnp.bfloat16)
    grad_up = lax.dot_general(
        act_second, grad_pre, contract_rows, preferred_element_type=jnp.float32
    )
    grad_up_bias = jnp.sum(grad_pre.astype(jnp.float32), axis=0)
    grad_act_two = lax.psum_scatter(
        lax.dot_general(
            grad_pre, up_weight, contract_cols, preferred_element_type=jnp.float32
        ).astype(jnp.bfloat16),
        "mp",
        scatter_dimension=0,
        tiled=True,
    ).astype(jnp.float32)
    cot_own = cotangent.astype(jnp.float32)
    resid_grad = cot_own + layer_back(grad_act_two * gain_b, normed_two, factor_two)
    grad_gain_two = jnp.sum(grad_act_two * normed_two, axis=0)
    grad_shift_two = jnp.sum(grad_act_two, axis=0)
    grad_down_bias = jnp.sum(cot_own, axis=0)
    branch_grad = resid_grad.astype(jnp.bfloat16)
    grad_out_bias = jnp.sum(branch_grad.astype(jnp.float32), axis=0)
    branch_all = lax.all_gather(branch_grad, "mp", axis=0, tiled=True)
    grad_out = lax.dot_general(
        context, branch_all, contract_rows, preferred_element_type=jnp.float32
    )
    grad_context = lax.dot_general(
        branch_all, out_weight, contract_cols, preferred_element_type=jnp.float32
    ).astype(jnp.bfloat16)
    grad_context = grad_context.reshape(groups, 5 * P_LO, heads_here, HD)

    def backward_group(packed):
        flag, group_q, group_k, group_v, group_total, group_grad = packed
        return lax.cond(
            flag, backward_two, backward_five, group_q, group_k, group_v, group_total, group_grad
        )

    grad_q, grad_k, grad_v = lax.map(
        backward_group, (single_big, queries, keys_all, values_all, log_totals, grad_context)
    )
    grad_rows = jnp.stack(
        [
            grad_q.reshape(rows, local_width),
            grad_k.reshape(rows, local_width),
            grad_v.reshape(rows, local_width),
        ]
    )
    grad_qkv = jnp.einsum("rd,cre->cde", act_first, grad_rows, preferred_element_type=jnp.float32)
    grad_qv = jnp.stack(
        [
            jnp.sum(grad_rows[0].astype(jnp.float32), axis=0),
            jnp.sum(grad_rows[2].astype(jnp.float32), axis=0),
        ]
    )
    grad_act_one = lax.psum_scatter(
        jnp.einsum("cre,cde->rd", grad_rows, qkv_weight, preferred_element_type=jnp.float32).astype(
            jnp.bfloat16
        ),
        "mp",
        scatter_dimension=0,
        tiled=True,
    ).astype(jnp.float32)
    normed_one = lax.dynamic_slice_in_dim(normed_first, offset, share, 0)
    factor_one = lax.dynamic_slice_in_dim(factor_first, offset, share, 0)
    input_grad = resid_grad + layer_back(grad_act_one * gain_a, normed_one, factor_one)
    grad_gain_one = jnp.sum(grad_act_one * normed_one, axis=0)
    grad_shift_one = jnp.sum(grad_act_one, axis=0)
    grad_gain_one, grad_shift_one, grad_gain_two, grad_shift_two, grad_out_bias, grad_down_bias = (
        lax.psum(
            (
                grad_gain_one,
                grad_shift_one,
                grad_gain_two,
                grad_shift_two,
                grad_out_bias,
                grad_down_bias,
            ),
            ("dp", "mp"),
        )
    )
    grad_qkv, grad_qv, grad_out, grad_up, grad_up_bias, grad_down = lax.psum(
        (grad_qkv, grad_qv, grad_out, grad_up, grad_up_bias, grad_down), "dp"
    )
    return (
        block_out,
        input_grad,
        grad_gain_one,
        grad_shift_one,
        grad_qkv,
        grad_qv,
        grad_out,
        grad_out_bias,
        grad_gain_two,
        grad_shift_two,
        grad_up,
        grad_up_bias,
        grad_down,
        grad_down_bias,
    )


def solution(mesh):
    return jax.shard_map(
        per_device,
        mesh=mesh,
        in_specs=(
            P("dp", None),
            P("dp"),
            P(),
            P(),
            P(None, None, "mp"),
            P(None, "mp"),
            P("mp", None),
            P(),
            P(),
            P(),
            P(None, "mp"),
            P("mp"),
            P("mp", None),
            P(),
            P(("dp", "mp"), None),
        ),
        out_specs=(
            P(("dp", "mp"), None),
            P(("dp", "mp"), None),
            P(),
            P(),
            P(None, None, "mp"),
            P(None, "mp"),
            P("mp", None),
            P(),
            P(),
            P(),
            P(None, "mp"),
            P("mp"),
            P("mp", None),
            P(),
        ),
        check_vma=False,
    )
```

profile of v0, /device:TPU:0, one launch (start us, length us, event | category | flops | bytes accessed | tf_op | source)
XLA Modules:
  0.0 480.8 jit_solution(2784213023636713431)
XLA Ops:
  20.3 7.2 %conditional.2 = (f32[3,980]{1,0:T(4,128)S(1)}, bf16[980,192]{0,1:T(8,128)(2,1)}) conditional(s32[]{:T(128)} %bitcast.51, (bf16[980,3,64]{0,2,1:T(8,128)(2,1)S(1)}, bf16[980,3,64]{0,2,1:T(8,128)(2,1)S(1)}, bf16[980,3,64]{0,2,1:T(8,128)(2,1)}) %tuple.85, (bf16[980,3,64]{0,2,1:T(8,128)(2,1)S(1)}, bf16[980,3,64]{0,2,1:T(8,128)(2,1)S(1)}, ...), branch_computations={%region_2.5_spmd, %region_5.10_spmd} | conditional | flops 517943328 | bytes 28636444 | solution.py:168
  27.5 2.9 convolution_convert_fusion.4
  31.6 50.8 %all-reduce.13.cloned.1.call-done = bf16[980,768]{1,0:T(8,128)(2,1)} async-done(((bf16[980,768]{1,0:T(8,128)(2,1)}), bf16[980,768]{1,0:T(8,128)(2,1)}) %all-reduce.13.cloned.1.call-update) | async-done | bytes 1505296 | tf_op jit(solution)/shard_map/psum | solution.py:173
  82.4 4.1 fusion.113
  89.9 3.1 fusion.108
  93.0 10.5 %all-gather.5.cloned.1.call-done = bf16[4,245,768]{2,1,0:T(8,128)(2,1)} async-done(((bf16[1,245,768]{2,1,0:T(8,128)(2,1)}), bf16[4,245,768]{2,1,0:T(8,128)(2,1)}) %all-gather.5.cloned.1.call-update) | async-done | bytes 1505296 | tf_op jit(solution)/shard_map/all_gather | solution.py:195
  103.5 2.9 reshape.412
  106.4 11.5 %convert_reduce_fusion.5 = (f32[768]{0:T(1024)}, bf16[980,768]{1,0:T(8,128)(2,1)S(1)}, f32[980,768]{1,0:T(8,128)}) fusion(f32[980,768]{1,0:T(8,128)} %fusion.108, f32[768]{0:T(1024)S(1)} %convert_element_type.307, bf16[980,768]{1,0:T(8,128)(2,1)} %reshape.412, bf16[768,768]{1,0:T(8,128)(2,1)S(1)} %copy-done), kind=kOutput, calls=%fused_computation.117 | convolution fusion | flops 1212502272 | bytes 10217472 | tf_op jit(solution)/shard_map/dot_general | solution.py:197
  119.1 2.5 convolution_convert_fusion.2
  121.6 18.8 %fusion.1 = bf16[248,768]{1,0:T(8,128)(2,1)} fusion(bf16[980,768]{1,0:T(8,128)(2,1)} %convolution_convert_fusion.2), kind=kCustom, calls=%all-reduce-scatter.1 | all-reduce-scatter fusion | flops 761857 | bytes 1886720
  144.4 3.8 concatenate.43
  150.5 2.4 convert_reduce_fusion.9
  154.6 9.9 %all-reduce.15.cloned.1.call-start = ((), (), s32[]{:S(2)}) async-start(), calls=%async_computation.3 | async-start | bytes 14155776 | tf_op jit(solution)/shard_map/psum | solution.py:279
  164.5 3.6 multiply_convert_fusion.3
  168.1 2.9 fusion.119
  171.8 2.9 fusion.107
  174.7 2.9 all-gather.7.cloned.1.call-done
  177.7 2.9 reshape.414
  180.6 2.8 fusion.118
  183.4 2.8 convolution_convert_fusion.5
  186.2 25.5 %conditional.3 = (bf16[1,980,192]{1,2,0:T(8,128)(2,1)}, f32[1,192]{1,0:T(1,128)S(1)}, bf16[1,980,192]{1,2,0:T(8,128)(2,1)}, bf16[1,980,192]{1,2,0:T(8,128)(2,1)}, f32[1,192]{1,0:T(1,128)S(1)}) conditional(s32[]{:T(128)} %bitcast.51, (bf16[980,3,64]{0,2,1:T(8,128)(2,1)S(1)}, bf16[980,3,64]{0,2,1:T(8,128)(2,1)S(1)}, f32[3,980]{1,0:T(4,128)S(1)}, ...), branch_computations={%region_17.21_spmd, %region_21.0_spmd} | conditional | flops 1282024704 | bytes 129332192 | solution.py:232
  198.1 5.8 %multiply_reduce_fusion.3 = (f32[3,784]{1,0:T(4,128)S(1)}, f32[3,784,784]{1,2,0:T(8,128)S(1)}) fusion(f32[3,784,784]{1,2,0:T(8,128)} %copy-done.1, f32[3,784]{1,0:T(4,128)S(1)} %slice.65, bf16[980,3,64]{0,2,1:T(8,128)(2,1)} %get-tuple-element.126, bf16[980,3,64]{0,2,1:T(8,128)(2,1)} %get-tuple-element.125), kind=kOutput, calls=%fused_computation.64 | convolution fusion | flops 243401424 | bytes 16512384 | tf_op jit(solution)/shard_map/while/body/eval_jaxpr/cond/branch_1_fun/blhe,bmhe->bhlm/dot_general | solution.py:49
  215.9 3.5 convolution_bitcast_fusion
  220.7 2.5 convolution_convert_fusion.3
  223.2 2.5 bitcast_convert_fusion
  225.8 30.5 %fusion.111 = (bf16[248,768]{1,0:T(8,128)(2,1)S(1)}, bf16[248,768]{1,0:T(8,128)(2,1)S(1)}) fusion(bf16[980,768]{1,0:T(8,128)(2,1)} %convolution_convert_fusion.3, bf16[980,768]{1,0:T(8,128)(2,1)} %bitcast_convert_fusion), kind=kCustom, calls=%all-reduce-scatter.3 | all-reduce-scatter fusion | flops 1523713 | bytes 3772928
  257.7 3.4 collective-permute-start
  261.2 29.6 %all-reduce.7 = (f32[2,192]{1,0:T(2,128)}, f32[768]{0:T(1024)}) all-reduce(f32[2,192]{1,0:T(2,128)S(1)} %pad_maximum_fusion.5, f32[768]{0:T(1024)S(1)} %copy-done.32), channel_id=1, replica_groups=mesh['dp'=8,'mp'=4] {'dp'}, use_global_device_ids=true, to_apply=%region_34.35 | all-reduce | flops 1152 | bytes 9216 | tf_op jit(solution)/shard_map/psum | solution.py:279
  294.6 40.8 %all-reduce.6 = (f32[768]{0:T(1024)}, f32[768]{0:T(1024)}, f32[768]{0:T(1024)}, f32[768]{0:T(1024)}, f32[768]{0:T(1024)}, /*index=5*/f32[768]{0:T(1024)}) all-reduce(f32[768]{0:T(1024)S(1)} %get-tuple-element.165, f32[768]{0:T(1024)S(1)} %get-tuple-element.170, f32[768]{0:T(1024)S(1)} %copy-done.29, ...), channel_id=1, replica_groups=mesh['dp'=8,'mp'=4] {'dp','mp'}, use_global_device_ids=true, to_apply=%region_30.31 | all-reduce | flops 4608 | bytes 36864 | tf_op jit(solution)/shard_map/psum | solution.py:267
  337.6 2.3 fusion.99
  339.9 127.3 %all-reduce.15.cloned.1.call-done = (f32[3,768,192]{1,2,0:T(8,128)}, f32[192,768]{1,0:T(8,128)}, f32[768,768]{1,0:T(8,128)}, f32[768,768]{1,0:T(8,128)}) async-done(((f32[3,768,192]{1,2,0:T(8,128)}, f32[192,768]{1,0:T(8,128)}, f32[768,768]{1,0:T(8,128)}, f32[768,768]{1,0:T(8,128)}), (f32[3,768,192]{1,2,0:T(8,128)}, f32[192,768]{1,0:T(8,128)}, f32[768,768]{1,0:T(8,128)}, ...) | async-done | bytes 7077904 | tf_op jit(solution)/shard_map/psum | solution.py:279
  467.2 2.9 copy.171
  (189 shorter events, 68.2 us)
Async XLA Ops:
  7.2 99.2 %copy-start = (bf16[768,768]{1,0:T(8,128)(2,1)S(1)}, bf16[768,768]{1,0:T(8,128)(2,1)}, u32[]{:S(2)}) copy-start(bf16[768,768]{1,0:T(8,128)(2,1)} %param.31) | copy-start | bytes 3538948
  7.2 5.3 %copy-start.5 = (bf16[980,768]{1,0:T(8,128)(2,1)S(1)}, bf16[980,768]{1,0:T(8,128)(2,1)}, u32[]{:S(2)}) copy-start(bf16[980,768]{1,0:T(8,128)(2,1)} %param.19) | copy-start | bytes 4515844
  7.2 75.2 %all-reduce.13.cloned.1.call-start = ((), (), s32[]{:S(2)}) async-start(), calls=%async_computation | async-start | bytes 3022848 | tf_op jit(solution)/shard_map/psum | solution.py:173
  7.3 5.3 %copy-start.48 = (bf16[3,768,192]{1,2,0:T(8,128)(2,1)S(1)}, bf16[3,768,192]{1,2,0:T(8,128)(2,1)}, u32[]{:S(2)}) copy-start(bf16[3,768,192]{1,2,0:T(8,128)(2,1)} %param.23) | copy-start | bytes 2654212
  8.8 5.1 %copy-start.31 = (f32[768]{0:T(1024)}, f32[768]{0:T(1024)S(1)}, u32[]{:S(2)}) copy-start(f32[768]{0:T(1024)S(1)} %convert_element_type.295) | copy-start | bytes 9220
  14.0 3.9 copy-start.44
  27.5 4.0 copy-start.39
  27.5 4.0 copy-start.40
  27.5 4.0 copy-start.41
  27.5 4.1 copy-start.42
  30.4 73.0 %all-gather.5.cloned.1.call-start = ((), (), s32[]{:S(2)}) async-start(), calls=%async_computation.1 | async-start | bytes 1904640 | tf_op jit(solution)/shard_map/all_gather | solution.py:195
  31.2 146.5 %all-gather.7.cloned.1.call-start = ((), (), s32[]{:S(2)}) async-start(), calls=%async_computation.2 | async-start | bytes 1904640 | tf_op jit(solution)/shard_map/all_gather | solution.py:221
  31.6 55.8 %copy-start.33 = (f32[768]{0:T(1024)}, f32[768]{0:T(1024)S(1)}, u32[]{:S(2)}) copy-start(f32[768]{0:T(1024)S(1)} %convert_element_type.305) | copy-start | bytes 9220
  106.4 12.7 %copy-start.47 = (bf16[768,768]{1,0:T(8,128)(2,1)S(1)}, bf16[768,768]{1,0:T(8,128)(2,1)}, u32[]{:S(2)}) copy-start(bf16[768,768]{1,0:T(8,128)(2,1)} %param.29) | copy-start | bytes 3538948
  119.1 24.0 %copy-start.45 = (u32[32]{0:T(128)S(1)}, u32[32]{0:T(128)}, u32[]{:S(2)}) copy-start(u32[32]{0:T(128)} %constant.147) | copy-start | bytes 388
  141.8 2.6 collective-permute-start.1
  154.6 312.6 %all-reduce.15.cloned.1.call-start = ((), (), s32[]{:S(2)}) async-start(), calls=%async_computation.3 | async-start | bytes 14155776 | tf_op jit(solution)/shard_map/psum | solution.py:279
  188.8 6.3 %copy-start.22 = (bf16[3,196,64]{1,2,0:T(8,128)(2,1)}, bf16[3,196,64]{1,2,0:T(8,128)(2,1)S(1)}, u32[]{:S(2)}) copy-start(bf16[3,196,64]{1,2,0:T(8,128)(2,1)S(1)} %convolution_convert_fusion.1) | copy-start | bytes 225796 | tf_op jit(solution)/shard_map/while/body/eval_jaxpr/cond
  196.1 7.8 %slice-start = ((s8[8429568]{0:T(1024)(128)(4,1)}), s8[4194304]{0:T(1024)(128)(4,1)S(1)}, s32[]{:S(2)}) async-start(s8[8429568]{0:T(1024)(128)(4,1)} %bitcast.152), calls=%async_computation.4 | async-start | bytes 8388608 | tf_op jit(solution)/shard_map/while/body/eval_jaxpr/cond
  198.1 5.8 %slice-start.1 = ((s8[8429568]{0:T(1024)(128)(4,1)}), s8[4194304]{0:T(1024)(128)(4,1)S(1)}, s32[]{:S(2)}) async-start(s8[8429568]{0:T(1024)(128)(4,1)} %bitcast.152), calls=%async_computation.5 | async-start | bytes 8388608 | tf_op jit(solution)/shard_map/while/body/eval_jaxpr/cond
  198.1 5.8 %slice-start.2 = ((s8[8429568]{0:T(1024)(128)(4,1)}), s8[40960]{0:T(1024)(128)(4,1)S(1)}, s32[]{:S(2)}) async-start(s8[8429568]{0:T(1024)(128)(4,1)} %bitcast.152), calls=%async_computation.6 | async-start | bytes 81920 | tf_op jit(solution)/shard_map/while/body/eval_jaxpr/cond
  211.7 7.6 %copy-start.35 = (f32[1,192]{1,0:T(1,128)}, f32[1,192]{1,0:T(1,128)S(1)}, u32[]{:S(2)}) copy-start(f32[1,192]{1,0:T(1,128)S(1)} %get-tuple-element.154) | copy-start | bytes 2308
  211.7 7.6 %copy-start.37 = (f32[1,192]{1,0:T(1,128)}, f32[1,192]{1,0:T(1,128)S(1)}, u32[]{:S(2)}) copy-start(f32[1,192]{1,0:T(1,128)S(1)} %get-tuple-element.153) | copy-start | bytes 2308
  225.7 35.4 %copy-start.36 = (f32[1,192]{1,0:T(1,128)S(1)}, f32[1,192]{1,0:T(1,128)}, u32[]{:S(2)}) copy-start(f32[1,192]{1,0:T(1,128)} %copy-done.35) | copy-start | bytes 2308
  225.7 35.4 %copy-start.38 = (f32[1,192]{1,0:T(1,128)S(1)}, f32[1,192]{1,0:T(1,128)}, u32[]{:S(2)}) copy-start(f32[1,192]{1,0:T(1,128)} %copy-done.37) | copy-start | bytes 2308
  225.7 35.5 %copy-start.32 = (f32[768]{0:T(1024)S(1)}, f32[768]{0:T(1024)}, u32[]{:S(2)}) copy-start(f32[768]{0:T(1024)} %get-tuple-element.189) | copy-start | bytes 9220
  225.7 68.9 %copy-start.28 = (f32[768]{0:T(1024)S(1)}, f32[768]{0:T(1024)}, u32[]{:S(2)}) copy-start(f32[768]{0:T(1024)} %get-tuple-element.169) | copy-start | bytes 9220
  225.8 68.9 %copy-start.29 = (f32[768]{0:T(1024)S(1)}, f32[768]{0:T(1024)}, u32[]{:S(2)}) copy-start(f32[768]{0:T(1024)} %get-tuple-element.192) | copy-start | bytes 9220
  225.8 68.9 %copy-start.30 = (f32[768]{0:T(1024)S(1)}, f32[768]{0:T(1024)}, u32[]{:S(2)}) copy-start(f32[768]{0:T(1024)} %get-tuple-element.217) | copy-start | bytes 9220
  256.2 81.4 %copy-start.8 = (f32[245,768]{1,0:T(8,128)S(1)}, f32[245,768]{1,0:T(8,128)}, u32[]{:S(2)}) copy-start(f32[245,768]{1,0:T(8,128)} %copy-done.7) | copy-start | bytes 2257924
  256.3 34.5 %collective-permute-start.2 = (bf16[9,768]{1,0:T(8,128)(2,1)S(1)}, bf16[9,768]{1,0:T(8,128)(2,1)S(1)}, u32[]{:S(2)}, u32[]{:S(2)}) collective-permute-start(bf16[9,768]{1,0:T(8,128)(2,1)S(1)} %slice.96), channel_id=1, source_target_pairs={{0,1},{1,2},{2,3},{4,5},{5,6},{6,7},{8,9},{9,10},{10,11},{12,13},{... | collective-permute-start | bytes 41480
  257.7 34.2 %collective-permute-start = (bf16[9,768]{1,0:T(8,128)(2,1)S(1)}, bf16[9,768]{1,0:T(8,128)(2,1)S(1)}, u32[]{:S(2)}, u32[]{:S(2)}) collective-permute-start(bf16[9,768]{1,0:T(8,128)(2,1)S(1)} %slice.94), channel_id=1, source_target_pairs={{0,1},{1,2},{2,3},{4,5},{5,6},{6,7},{8,9},{9,10},{10,11},{12,13},{... | collective-permute-start | bytes 41480
  (25 other events, 55.6 us)
Sparse Core Ops, SparseCore 0:
  30.5 51.8 all-reduce.12
  84.0 19.3 all-gather.4
  154.7 22.9 all-gather.6
  219.5 247.6 all-reduce.14
where the time goes:
time: 489 us; the launch traced here: 481 us
  waiting for transfers between devices  192 us (39%)
  blocking collectives  120 us (25%)
  matrix products  61.3 us (13%)
  other arithmetic  36.9 us (8%)
  local copies, waits for them, and re-layouts  36.8 us (8%)
  between operations  16.7 us (3%)
  starting transfers between devices  16.5 us (3%)
    psum x1, waiting for transfers between devices, per_device(): lax.psum((grad_qkv, grad_qv, grad_out, grad_up, grad_up_bias, grad_down),...  127 us
    psum x1, waiting for transfers between devices, per_device(): lax.psum(jnp.dot(context, out_weight, preferred_element_type=jnp.float32)...  50.8 us
    unnamed x2, blocking collectives  49.3 us
    psum x1, blocking collectives, per_device(): lax.psum((grad_gain_one, grad_shift_one, grad_gain_two, grad_shift_two, g...  40.8 us
    unnamed x93, local copies, waits for them, and re-layouts  30.2 us
    psum x1, blocking collectives, per_device(): lax.psum((grad_qkv, grad_qv, grad_out, grad_up, grad_up_bias, grad_down),...  29.6 us
    dot_general x1, matrix products, per_device(): lax.dot_general(cot_all, down_weight, contract_cols, preferred_element_ty...  11.5 us
    all_gather x1, waiting for transfers between devices, per_device(): cot_all = lax.all_gather(cotangent, 'mp', axis=0, tiled=True)  10.5 us
  transfers between devices with their start and end apart: 7, of which 4 were waited for; matrix products, arithmetic and copies ran while one was open for 13% of the time, Pallas kernels for 0%

commit v1 on v0

v1 whole, which is shorter than its diff:
```python
import functools

import jax
import jax.numpy as jnp
from jax import lax
from jax.experimental import pallas as pl
from jax.experimental.pallas import tpu as pltpu
from jax.sharding import PartitionSpec as P

f32, bf16, i32 = jnp.float32, jnp.bfloat16, jnp.int32
MESH = pl.DeviceIdType.MESH
NN = (((1,), (0,)), ((), ()))
NT = (((1,), (1,)), ((), ()))
TN = (((0,), (0,)), ((), ()))
HD = 64
P_LO = 196
EPSILON = 1e-06
B = 256
TOP = 832
BIG = 4 * P_LO


def dot(left, right, dims):
    return lax.dot_general(left, right, dims, preferred_element_type=f32)


def rows(start, size=B):
    return pl.ds(pl.multiple_of(start * size, size), size)


def layer_hat(values):
    center = values - jnp.mean(values, axis=1, keepdims=True)
    factor = lax.rsqrt(jnp.mean(center * center, axis=1, keepdims=True) + EPSILON)
    return center * factor, factor


def layer_back(grad_hat, normed, factor):
    first = jnp.mean(grad_hat, axis=1, keepdims=True)
    second = jnp.mean(grad_hat * normed, axis=1, keepdims=True)
    return factor * (grad_hat - first - normed * second)


def column_sum(values):
    return jnp.sum(values, axis=0, keepdims=True)


def remote(src, dst, send, recv, device):
    return pltpu.make_async_remote_copy(
        src_ref=src, dst_ref=dst, send_sem=send, recv_sem=recv, device_id=device, device_id_type=MESH
    )


class Gather:
    def __init__(self, place, view, send, recv):
        self.me, self.core, self.across = place
        self.view, self.send, self.recv = view, send, recv

    def copy(self, slot, k, device):
        return remote(self.view(slot), self.view(slot), self.send(k), self.recv(k), device)

    def start(self):
        self.copy(self.me, 1, self.across).start()
        self.copy(self.me, 0, self.core).start()

    def forward(self):
        slot = self.me ^ 2
        self.copy(slot, 1, self.across).wait_recv()
        self.copy(slot, 2, self.core).start()

    def land_core(self):
        self.copy(self.me ^ 1, 0, self.core).wait_recv()

    def land_far(self):
        self.copy(self.me ^ 3, 2, self.core).wait_recv()

    def close(self):
        for k in range(3):
            self.copy(self.me, k, self.core).wait_send()


class Scatter:
    def __init__(self, place, out, both, far, own, send, recv):
        self.me, self.core, self.across = place
        self.out, self.both, self.far, self.own = out, both, far, own
        self.send, self.recv = send, recv

    def copy(self, k):
        src = self.out.at[k]
        dst = self.far if k == 1 else self.both.at[k // 2]
        return remote(src, dst, self.send.at[k], self.recv.at[k], self.across if k == 1 else self.core)

    def step(self, i, value):
        @pl.when(i == 0)
        def _():
            self.out[0] = value().astype(bf16)
            self.copy(0).start()

        @pl.when(i == 1)
        def _():
            self.copy(0).wait_recv()
            self.out[1] = (value() + self.both[0].astype(f32)).astype(bf16)
            self.copy(1).start()

        @pl.when(i == 2)
        def _():
            self.out[2] = value().astype(bf16)
            self.copy(2).start()

        @pl.when(i == 3)
        def _():
            self.own[...] = value()

    def finish(self):
        self.copy(2).wait_recv()
        self.copy(1).wait_recv()
        total = self.own[...] + self.both[1].astype(f32) + self.far[...].astype(f32)
        for k in range(3):
            self.copy(k).wait_send()
        return total


class Reduce:
    def __init__(self, spot, part, ybuf, zbuf, whole, send, recv):
        self.zi, self.yi, self.ypeer, self.zpeers = spot
        self.part, self.ybuf, self.zbuf, self.whole = part, ybuf, zbuf, whole
        self.send, self.recv = send, recv
        self.quarter = part.shape[1] // 4

    def piece(self, ref, half, quarter):
        return ref.at[half, pl.ds(pl.multiple_of(quarter * self.quarter, 16), self.quarter)]

    def copy_y(self):
        return remote(self.part.at[1 - self.yi], self.ybuf, self.send.at[0], self.recv.at[0], self.ypeer)

    def copy_z(self, j):
        src = self.piece(self.part, self.yi, self.zi ^ j)
        return remote(src, self.zbuf.at[j - 1], self.send.at[j], self.recv.at[j], self.zpeers[j - 1])

    def copy_back(self, j, quarter):
        view = self.piece(self.whole, self.yi, quarter)
        return remote(view, view, self.send.at[3 + j], self.recv.at[3 + j], self.zpeers[j - 1])

    def copy_over(self, j, half):
        view = self.piece(self.whole, half, self.zi ^ j)
        return remote(view, view, self.send.at[7 + j], self.recv.at[7 + j], self.ypeer)

    def one(self):
        self.copy_y().start()

    def two(self):
        self.copy_y().wait_recv()

        def add(q, carry):
            span = pl.ds(pl.multiple_of(q * self.quarter, 16), self.quarter)
            total = self.part[self.yi, span].astype(f32) + self.ybuf[span].astype(f32)
            self.part[self.yi, span] = total.astype(bf16)
            return carry

        lax.fori_loop(0, 4, add, 0)
        for j in (3, 2, 1):
            self.copy_z(j).start()

    def three(self):
        span = pl.ds(pl.multiple_of(self.zi * self.quarter, 16), self.quarter)
        total = self.part[self.yi, span].astype(f32)
        for j in (1, 2, 3):
            self.copy_z(j).wait_recv()
            total = total + self.zbuf[j - 1].astype(f32)
        self.whole[self.yi, span] = total.astype(bf16)
        for j in (3, 2, 1):
            self.copy_back(j, self.zi).start()
        self.copy_over(0, self.yi).start()

    def four(self):
        for j in (1, 2, 3):
            self.copy_back(j, self.zi ^ j).wait_recv()
            self.copy_over(j, self.yi).start()

    def five(self):
        for j in range(4):
            self.copy_over(j, 1 - self.yi).wait_recv()

    def close(self):
        self.copy_y().wait_send()
        for j in (1, 2, 3):
            self.copy_z(j).wait_send()
            self.copy_back(j, self.zi).wait_send()
        for j in range(4):
            self.copy_over(j, self.yi).wait_send()


def layer_kernel(
    x_ref, ids_ref, vec_ref, wqkv_ref, wo_ref, wup_ref, wdn_ref, cot_ref,
    block_ref, input_ref, sums_ref, down_hbm, up_hbm, out_hbm, qkv_hbm,
    xp, stage, a1, keys, values, keys_t, values_t, qz_t, qz, kid, qid, probs, probs_last, rinv, ctx_t, ctx_all,
    wo_all, cot_all, a2, gate, du, do_all, dcz_t, dcz, delta, dq, dk, dv, dkb, dvb, own,
    rs_out, rs_both, rs_far, ms_out, ms_both, ms_far, m_own,
    gd_part, gd_y, gd_z, gd_all, gu_part, gu_y, gu_z, gu_all,
    go_part, go_y, go_z, go_all, gq_part, gq_y, gq_z, gq_all,
    acc, v_mp, v_y, v_z,
    wo_send, wo_recv, cot_send, cot_recv, ctx_send, ctx_recv, do_send, do_recv,
    rs_send, rs_recv, ms_send, ms_recv, rt_send, rt_recv,
    gd_send, gd_recv, gu_send, gu_recv, go_send, go_recv, gq_send, gq_recv,
    v_send, v_recv, local_sem,
):
    dp, me = lax.axis_index("dp"), lax.axis_index("mp")
    core, across, diagonal = (dp, me ^ 1), (dp, me ^ 2), (dp, me ^ 3)
    yi, zi = dp & 1, (dp >> 1) & 3
    ypeer = (dp ^ 1, me)
    zpeers = [(dp ^ (2 * j), me) for j in (1, 2, 3)]
    place = (me, core, across)
    spot = (zi, yi, ypeer, zpeers)
    share = cot_ref.shape[0]

    barrier = pltpu.get_barrier_semaphore()
    partners = [core, across, diagonal, ypeer] + zpeers
    for partner in partners:
        pl.semaphore_signal(barrier, inc=1, device_id=partner, device_id_type=MESH)

    def vec(r, width=None):
        return vec_ref[r : r + 1, :] if width is None else vec_ref[r : r + 1, width[0] : width[1]]

    stage[240:256, :] = jnp.zeros((16, 768), f32)
    stage[0:share, :] = cot_ref[...].astype(f32)
    cot_all[rows(me), :] = stage[0:B, :].astype(bf16)
    wo_all[me] = wo_ref[...]
    acc[...] = jnp.zeros(acc.shape, f32)
    pl.semaphore_wait(barrier, len(partners))

    gather_wo = Gather(place, lambda s: wo_all.at[s], lambda k: wo_send.at[k], lambda k: wo_recv.at[k])
    gather_cot = Gather(place, lambda s: cot_all.at[rows(s)], lambda k: cot_send.at[k], lambda k: cot_recv.at[k])
    gather_wo.start()
    gather_cot.start()

    row_in = lax.broadcasted_iota(i32, (B, 768), 0)
    for s in range(4):
        first = s * share // 16 * 16
        last = min(first + 272, 4 * share)
        stage[0 : last - first, :] = x_ref[first:last, :].astype(f32)
        moved = stage[s * share - first : s * share - first + B, :]
        xp[s * B : (s + 1) * B, :] = jnp.where(row_in < share, moved, 0.0).astype(bf16)

    two_images = (ids_ref[0] == ids_ref[BIG - 1]).astype(i32)

    def image_of(index, shard, pad):
        place_of = index + shard * share
        small = jnp.zeros_like(index)
        for k in range(1, 5):
            small = small + (place_of >= k * P_LO).astype(i32)
        large = (place_of >= BIG).astype(i32)
        image = small * (1 - two_images) + large * two_images
        return jnp.where(index < share, image, pad)

    def images(s, carry):
        kid[rows(s), :] = image_of(lax.broadcasted_iota(i32, (B, B), 0), s, -1)
        qid[s] = image_of(lax.broadcasted_iota(i32, (8, B), 1), s, -2)
        qz_t[s] = jnp.zeros(qz_t.shape[1:], bf16)
        return carry

    lax.fori_loop(0, 4, images, 0)

    lane_head = lax.broadcasted_iota(i32, (B, 192), 1) // HD

    def project(s, carry):
        span = rows(s)
        hat, _ = layer_hat(xp[span, :].astype(f32))
        act = (hat * vec(0) + vec(1)).astype(bf16)
        a1[span, :] = act
        q = (dot(act, wqkv_ref[0], NN) + vec(7, (0, 192))).astype(bf16)
        k = dot(act, wqkv_ref[1], NN).astype(bf16)
        v = (dot(act, wqkv_ref[2], NN) + vec(7, (256, 448))).astype(bf16)
        keys[span, :] = k
        values[span, :] = v
        keys_t[:, span] = k.T
        values_t[:, span] = v.T
        q = q.astype(f32) * HD**-0.5
        qt = q.astype(bf16).T
        for h in range(3):
            qz_t[s, h * HD : (h + 1) * HD, h * B : (h + 1) * B] = qt[h * HD : (h + 1) * HD, :]
            qz[s, h * B : (h + 1) * B, :] = jnp.where(lane_head == h, q, 0.0).astype(bf16)
        return carry

    lax.fori_loop(0, 4, project, 0)

    def gather_ctx(s):
        return Gather(
            place, lambda j: ctx_all.at[j, s], lambda k: ctx_send.at[s, k], lambda k: ctx_recv.at[s, k]
        )

    def attend(s, h, low, high, qlow, qhigh, store):
        lanes = pl.ds(pl.multiple_of(h * B + qlow, 128), qhigh - qlow)
        scores = dot(keys[low:high, :], qz_t[s, :, lanes], NN)
        same = kid[low:high, qlow:qhigh] == qid[s, 0:1, qlow:qhigh]
        scores = jnp.where(same, scores, -1e30)
        top = jnp.max(scores, axis=0, keepdims=True)
        weights = jnp.exp(scores - top)
        inverse = 1.0 / jnp.sum(weights, axis=0, keepdims=True)
        weights = weights.astype(bf16)
        store(lanes, weights)
        rinv[s, h, 0:1, qlow:qhigh] = inverse
        head = pl.ds(pl.multiple_of(h * HD, HD), HD)
        return (dot(values_t[head, low:high], weights, NN) * inverse).astype(bf16)

    def send_ctx(s):
        span = rows(s)
        block = ctx_t[:, span]
        ctx_all[me, s, 0:B, :] = block[0:128, :].T
        last = jnp.concatenate([block[128:192, 0:128], block[128:192, 128:256]], axis=0)
        ctx_all[me, s, B : B + 128, :] = last.T
        gather_ctx(s).start()

    def attend_top(s, carry):
        def head(h, inner):
            def store(lanes, weights):
                probs[s, :, lanes] = weights

            here = pl.ds(pl.multiple_of(h * HD, HD), HD)
            ctx_t[here, rows(s)] = attend(s, h, 0, TOP, 0, B, store)
            return inner

        lax.fori_loop(0, 3, head, 0)
        send_ctx(s)

        @pl.when(s == 1)
        def _():
            gather_wo.forward()

        @pl.when(s == 2)
        def _():
            gather_cot.forward()

        return carry

    lax.fori_loop(0, 3, attend_top, 0)

    def attend_last(h, carry):
        here = pl.ds(pl.multiple_of(h * HD, HD), HD)

        def store_left(lanes, weights):
            probs_last[:, lanes] = weights

        def store_right(lanes, weights):
            probs_last[0:768, lanes] = jnp.zeros((768, 128), bf16)
            probs_last[768:1024, lanes] = weights

        ctx_t[here, 768:896] = attend(3, h, 0, 1024, 0, 128, store_left)
        ctx_t[here, 896:1024] = attend(3, h, 768, 1024, 128, 256, store_right)
        return carry

    lax.fori_loop(0, 3, attend_last, 0)
    send_ctx(3)

    gather_wo.land_core()
    gather_wo.land_far()
    gather_cot.land_core()
    gather_cot.land_far()
    for s in range(4):
        gather_ctx(s).forward()

    sum_in = Scatter(place, rs_out, rs_both, rs_far, own, rs_send, rs_recv)
    zeros_w = jnp.zeros((HD, 768), bf16)

    def middle(i, carry):
        s = me ^ (3 - i)
        span = rows(s)
        ctx = gather_ctx(s)
        ctx.land_core()
        ctx.land_far()
        left = jnp.concatenate([ctx_all[j, s, 0:B, :] for j in range(4)], axis=1)
        last = jnp.concatenate([ctx_all[j, s, B : B + 128, :] for j in range(4)], axis=1)
        w_left = jnp.concatenate([wo_all[j, 0:128, :] for j in range(4)], axis=0)
        w_tail = [wo_all[j, 128:192, :] for j in range(4)]
        w_upper = jnp.concatenate([piece for w in w_tail for piece in (w, zeros_w)], axis=0)
        w_lower = jnp.concatenate([piece for w in w_tail for piece in (zeros_w, w)], axis=0)
        branch = dot(left, w_left, NN) + jnp.concatenate(
            [dot(last, w_upper, NN), dot(last, w_lower, NN)], axis=0
        )
        h = xp[span, :].astype(f32) + (branch + vec(2))

        @pl.when(i == 3)
        def _():
            block_ref[...] = h

        hat, _ = layer_hat(h)
        stage[0:B, :] = hat
        act = (hat * vec(3) + vec(4)).astype(bf16)
        a2[span, :] = act
        u = dot(act, wup_ref[...], NN) + vec(5)
        cdf = 0.5 * (1.0 + lax.erf(u * 0.7071067811865476))
        gate[span, :] = (u * cdf).astype(bf16)
        slope = cdf + u * (0.3989422804014327 * jnp.exp(-0.5 * (u * u)))
        grad_u = (dot(cot_all[span, :], wdn_ref[...], NT) * slope).astype(bf16)
        du[span, :] = grad_u
        acc[8:9, :] += column_sum(grad_u.astype(f32))
        grad_act = dot(grad_u, wup_ref[...], NT)
        acc[2:3, :] += column_sum(grad_act * stage[0:B, :])
        acc[3:4, :] += column_sum(grad_act)
        own[...] = grad_act
        sum_in.step(i, lambda: own[...])
        return carry

    lax.fori_loop(0, 4, middle, 0)

    def grad_tiles(part, left, right, width):
        def tile(i, carry):
            piece = dot(left[:, rows(i, width)], right[...], TN).astype(bf16)
            part[0, rows(i, width), :] = piece[:, 0:384]
            part[1, rows(i, width), :] = piece[:, 384:768]
            return carry

        lax.fori_loop(0, 768 // width, tile, 0)

    reduce_down = Reduce(spot, gd_part, gd_y, gd_z, gd_all, gd_send, gd_recv)
    reduce_up = Reduce(spot, gu_part, gu_y, gu_z, gu_all, gu_send, gu_recv)
    reduce_out = Reduce(spot, go_part, go_y, go_z, go_all, go_send, go_recv)
    reduce_qkv = Reduce(spot, gq_part, gq_y, gq_z, gq_all, gq_send, gq_recv)

    grad_tiles(gd_part, gate, cot_all, B)
    reduce_down.one()
    grad_tiles(gu_part, a2, du, B)
    reduce_up.one()

    grad_act = sum_in.finish()
    hat, factor = layer_hat(block_ref[...])
    cot_own = cot_all[rows(me), :].astype(f32)
    grad_h = cot_own + layer_back(grad_act * vec(3), hat, factor)
    input_ref[...] = grad_h
    grad_branch = grad_h.astype(bf16)
    do_all[rows(me), :] = grad_branch
    gather_do = Gather(place, lambda s: do_all.at[rows(s)], lambda k: do_send.at[k], lambda k: do_recv.at[k])
    gather_do.start()
    acc[4:5, :] = column_sum(grad_branch.astype(f32))
    acc[5:6, :] = column_sum(cot_own)

    sum_out = Scatter(place, ms_out, ms_both, ms_far, m_own, ms_send, ms_recv)

    def project_down(i, carry):
        s = me ^ (3 - i)
        m_own[...] = dot(gate[rows(s), :], wdn_ref[...], NN)
        sum_out.step(i, lambda: m_own[...])
        return carry

    lax.fori_loop(0, 4, project_down, 0)
    reduce_down.two()

    dk[...] = jnp.zeros(dk.shape, f32)
    dv[...] = jnp.zeros(dv.shape, f32)

    def back_head(s, h, low, high, qlow, qhigh, ref):
        lanes = pl.ds(pl.multiple_of(h * B + qlow, 128), qhigh - qlow)
        head = pl.ds(pl.multiple_of(h * HD, HD), HD)
        weights = ref[low:high, lanes]
        grad_probs = dot(values[low:high, :], dcz_t[:, lanes], NN)
        grad_scores = weights.astype(f32) * (grad_probs - delta[h, 0:1, qlow:qhigh])
        grad_scores = grad_scores.astype(bf16)
        ref[low:high, lanes] = grad_scores
        return dot(keys_t[head, low:high], grad_scores, NN)

    def back_block(i, carry):
        s = me ^ i
        span = rows(s)

        @pl.when(i == 1)
        def _():
            gather_do.land_core()

        @pl.when(i == 2)
        def _():
            gather_do.forward()
            reduce_up.two()

        @pl.when(i == 3)
        def _():
            gather_do.land_far()
            reduce_down.three()

        grad_ctx = dot(wo_ref[...], do_all[span, :], NT).astype(bf16).astype(f32)
        for h in range(3):
            here = slice(h * HD, (h + 1) * HD)
            scaled = (grad_ctx[here, :] * rinv[s, h, 0:1, :]).astype(bf16)
            delta[h, 0:1, :] = column_sum(scaled.astype(f32) * ctx_t[here, span].astype(f32))
            dcz_t[here, h * B : (h + 1) * B] = scaled
            turned = jnp.concatenate([scaled, jnp.zeros((HD, B), bf16)], axis=0).T.astype(f32)
            wide = jnp.concatenate([turned, turned], axis=1)[:, 0:192]
            if h == 1:
                wide = pltpu.roll(jnp.concatenate([turned, jnp.zeros((B, 128), f32)], axis=1), HD, 1)[:, 0:192]
            dcz[h * B : (h + 1) * B, :] = jnp.where(lane_head == h, wide, 0.0).astype(bf16)

        @pl.when(s != 3)
        def _():
            dv[0:TOP, :] += dot(probs[s], dcz[...], NN)
            ref = probs.at[s]

            def head(h, inner):
                grad = back_head(s, h, 0, TOP, 0, B, ref)
                stage[pl.ds(pl.multiple_of(h * HD, HD), HD), 0:B] = grad
                return inner

            lax.fori_loop(0, 3, head, 0)
            dk[0:TOP, :] += dot(probs[s], qz[s], NN)

        @pl.when(s == 3)
        def _():
            dv[...] += dot(probs_last[...], dcz[...], NN)

            def head(h, inner):
                here = pl.ds(pl.multiple_of(h * HD, HD), HD)
                stage[here, 0:128] = back_head(s, h, 0, 1024, 0, 128, probs_last)
                stage[here, 128:256] = back_head(s, h, 768, 1024, 128, 256, probs_last)
                return inner

            lax.fori_loop(0, 3, head, 0)
            dk[...] += dot(probs_last[...], qz[s], NN)

        dq[span, :] = (stage[0:192, 0:B] * HD**-0.5).T.astype(bf16)
        return carry

    dcz_t[...] = jnp.zeros(dcz_t.shape, bf16)
    lax.fori_loop(0, 4, back_block, 0)

    grad_out = dot(ctx_t[...], do_all[...], NN).astype(bf16)
    go_part[0] = grad_out[:, 0:384]
    go_part[1] = grad_out[:, 384:768]
    reduce_out.one()
    reduce_up.three()

    dkb[...] = dk[...].astype(bf16)
    dvb[...] = dv[...].astype(bf16)
    for t, ref in enumerate((dq, dkb, dvb)):
        piece = dot(ref[...], a1[...], TN).astype(bf16)
        gq_part[0, t * 192 : (t + 1) * 192, :] = piece[:, 0:384]
        gq_part[1, t * 192 : (t + 1) * 192, :] = piece[:, 384:768]
    reduce_qkv.one()
    acc[9:10, 0:192] = column_sum(dq[...].astype(f32))
    acc[9:10, 256:448] = column_sum(dvb[...].astype(f32))

    sum_first = Scatter(place, rs_out, rs_both, rs_far, own, rt_send, rt_recv)

    def project_back(i, carry):
        s = me ^ (3 - i)
        span = rows(s)
        grad = dot(dq[span, :], wqkv_ref[0], NT)
        grad = grad + dot(dkb[span, :], wqkv_ref[1], NT)
        grad = grad + dot(dvb[span, :], wqkv_ref[2], NT)
        hat, _ = layer_hat(xp[span, :].astype(f32))
        acc[0:1, :] += column_sum(grad * hat)
        acc[1:2, :] += column_sum(grad)
        own[...] = grad
        sum_first.step(i, lambda: own[...])
        return carry

    lax.fori_loop(0, 4, project_back, 0)

    v_mp[me] = acc[...]
    v_copies = [remote(v_mp.at[me], v_mp.at[me], v_send.at[j - 1], v_recv.at[j - 1], (dp, me ^ j)) for j in (1, 2, 3)]
    v_lands = [remote(v_mp.at[me ^ j], v_mp.at[me ^ j], v_send.at[j - 1], v_recv.at[j - 1], (dp, me ^ j)) for j in (1, 2, 3)]
    for copy in v_copies:
        copy.start()
    reduce_out.two()
    reduce_qkv.two()
    for copy in v_lands:
        copy.wait_recv()
    acc[0:8, :] = v_mp[0, 0:8, :] + v_mp[1, 0:8, :] + v_mp[2, 0:8, :] + v_mp[3, 0:8, :]
    vy_copy = remote(acc, v_y, v_send.at[3], v_recv.at[3], ypeer)
    vy_copy.start()
    reduce_down.four()
    reduce_up.four()
    reduce_out.three()
    vy_copy.wait_recv()
    v_z[zi] = acc[...] + v_y[...]
    vz_copies = [remote(v_z.at[zi], v_z.at[zi], v_send.at[3 + j], v_recv.at[3 + j], zpeers[j - 1]) for j in (1, 2, 3)]
    vz_lands = [remote(v_z.at[zi ^ j], v_z.at[zi ^ j], v_send.at[3 + j], v_recv.at[3 + j], zpeers[j - 1]) for j in (1, 2, 3)]
    for copy in vz_copies:
        copy.start()
    reduce_qkv.three()

    block_ref[...] = block_ref[...] + (sum_out.finish() + vec(6))
    reduce_down.five()
    save_down = pltpu.make_async_copy(gd_all, down_hbm, local_sem.at[0])
    save_down.start()
    reduce_up.five()
    save_up = pltpu.make_async_copy(gu_all, up_hbm, local_sem.at[1])
    save_up.start()
    reduce_out.four()
    for copy in vz_lands:
        copy.wait_recv()
    sums_ref[...] = v_z[0] + v_z[1] + v_z[2] + v_z[3]

    grad_act = sum_first.finish()
    hat, factor = layer_hat(xp[rows(me), :].astype(f32))
    input_ref[...] = input_ref[...] + layer_back(grad_act * vec(0), hat, factor)

    reduce_out.five()
    save_out = pltpu.make_async_copy(go_all, out_hbm, local_sem.at[2])
    save_out.start()
    reduce_qkv.four()
    reduce_qkv.five()
    save_qkv = pltpu.make_async_copy(gq_all, qkv_hbm, local_sem.at[3])
    save_qkv.start()

    for copy in v_copies + [vy_copy] + vz_copies:
        copy.wait_send()
    for gather in [gather_wo, gather_cot, gather_do] + [gather_ctx(s) for s in range(4)]:
        gather.close()
    for reduce in (reduce_down, reduce_up, reduce_out, reduce_qkv):
        reduce.close()
    for save in (save_down, save_up, save_out, save_qkv):
        save.wait()


def finish_kernel(
    block_ref, input_ref, sums_ref, down_ref, up_ref, out_ref, qkv_ref,
    block_out, input_grad, gain_first, shift_first, grad_qkv, grad_qv, grad_out, out_bias, gain_second, shift_second,
    grad_up, up_bias, grad_down, down_bias,
):
    share = block_out.shape[0]
    block_out[...] = block_ref[0:share, :]
    input_grad[...] = input_ref[0:share, :]
    for r, ref in enumerate((gain_first, shift_first, gain_second, shift_second, out_bias, down_bias)):
        ref[...] = sums_ref[r, :]
    up_bias[...] = sums_ref[8, :]
    grad_qv[0:1, :] = sums_ref[9:10, 0:192]
    grad_qv[1:2, :] = sums_ref[9:10, 256:448]
    for source, target in ((down_ref, grad_down), (up_ref, grad_up), (out_ref, grad_out)):
        for half in range(2):
            target[:, half * 384 : (half + 1) * 384] = source[half].astype(f32)
    for t in range(3):
        for half in range(2):
            turned = qkv_ref[half, t * 192 : (t + 1) * 192, :].astype(f32).T
            grad_qkv[t, half * 384 : (half + 1) * 384, :] = turned


def per_device(
    inputs, image_of_row, gain_first, shift_first, qkv_weight, qv_bias, out_weight, out_bias, gain_second,
    shift_second, up_weight, up_bias, down_weight, down_bias, cotangent,
):
    qv_row = jnp.concatenate([jnp.pad(qv_bias[0], (0, 64)), jnp.pad(qv_bias[1], (0, 320))])
    packed = jnp.stack(
        [gain_first, shift_first, out_bias, gain_second, shift_second, up_bias, down_bias, qv_row]
    ).astype(f32)
    share = cotangent.shape[0]
    vmem, smem, anyspace = (pl.BlockSpec(memory_space=m) for m in (pltpu.VMEM, pltpu.SMEM, pl.ANY))

    def shape(*dims, dtype=bf16):
        return pltpu.VMEM(dims, dtype)

    def job(n):
        return [shape(2, n, 384), shape(n, 384), shape(3, n // 4, 384), shape(2, n, 384)]

    scratch = [
        shape(1024, 768), shape(272, 768, dtype=f32), shape(1024, 768),
        shape(1024, 192), shape(1024, 192), shape(192, 1024), shape(192, 1024),
        shape(4, 192, 768), shape(4, 768, 192),
        shape(1024, B, dtype=i32), shape(4, 8, B, dtype=i32),
        shape(3, TOP, 768), shape(1024, 768), shape(4, 3, 8, B, dtype=f32),
        shape(192, 1024), shape(4, 4, 384, 128), shape(4, 192, 768), shape(1024, 768),
        shape(1024, 768), shape(1024, 768), shape(1024, 768), shape(1024, 768),
        shape(192, 768), shape(768, 192), shape(3, 8, B, dtype=f32),
        shape(1024, 192), shape(1024, 192, dtype=f32), shape(1024, 192, dtype=f32),
        shape(1024, 192), shape(1024, 192), shape(B, 768, dtype=f32),
        shape(3, B, 768), shape(2, B, 768), shape(B, 768),
        shape(3, B, 768), shape(2, B, 768), shape(B, 768), shape(B, 768, dtype=f32),
        *job(768), *job(768), *job(192), *job(576),
        shape(16, 768, dtype=f32), shape(4, 16, 768, dtype=f32), shape(16, 768, dtype=f32), shape(4, 16, 768, dtype=f32),
    ]
    dma = pltpu.SemaphoreType.DMA
    scratch += [dma((3,))] * 4 + [dma((4, 3))] * 2 + [dma((3,))] * 8 + [dma((11,))] * 8 + [dma((7,))] * 2 + [dma((4,))]
    results = pl.pallas_call(
        layer_kernel,
        out_shape=[
            jax.ShapeDtypeStruct((B, 768), f32),
            jax.ShapeDtypeStruct((B, 768), f32),
            jax.ShapeDtypeStruct((16, 768), f32),
            jax.ShapeDtypeStruct((2, 768, 384), bf16),
            jax.ShapeDtypeStruct((2, 768, 384), bf16),
            jax.ShapeDtypeStruct((2, 192, 384), bf16),
            jax.ShapeDtypeStruct((2, 576, 384), bf16),
        ],
        in_specs=[vmem, smem] + [vmem] * 6,
        out_specs=[vmem] * 3 + [anyspace] * 4,
        scratch_shapes=scratch,
        compiler_params=pltpu.CompilerParams(
            collective_id=0, has_side_effects=True, vmem_limit_bytes=60 * 2**20
        ),
        name="layer",
    )(inputs, image_of_row, packed, qkv_weight, out_weight, up_weight, down_weight, cotangent)

    def out(*dims):
        return jax.ShapeDtypeStruct(dims, f32)

    return tuple(
        pl.pallas_call(
            finish_kernel,
            out_shape=[
                out(share, 768), out(share, 768), out(768), out(768), out(3, 768, 192), out(2, 192), out(192, 768),
                out(768), out(768), out(768), out(768, 768), out(768), out(768, 768), out(768),
            ],
            in_specs=[vmem] * 7,
            out_specs=[vmem] * 14,
            compiler_params=pltpu.CompilerParams(vmem_limit_bytes=32 * 2**20),
            name="finish",
        )(*results)
    )


def solution(mesh):
    return jax.shard_map(
        per_device,
        mesh=mesh,
        in_specs=(
            P("dp", None),
            P("dp"),
            P(),
            P(),
            P(None, None, "mp"),
            P(None, "mp"),
            P("mp", None),
            P(),
            P(),
            P(),
            P(None, "mp"),
            P("mp"),
            P("mp", None),
            P(),
            P(("dp", "mp"), None),
        ),
        out_specs=(
            P(("dp", "mp"), None),
            P(("dp", "mp"), None),
            P(),
            P(),
            P(None, None, "mp"),
            P(None, "mp"),
            P("mp", None),
            P(),
            P(),
            P(),
            P(None, "mp"),
            P("mp"),
            P("mp", None),
            P(),
        ),
        check_vma=False,
    )
```

time: 489 us -> 171 us (0.35); the launches traced: 481 us -> 171 us
  waiting for transfers between devices: 192 us -> 0 us
  Pallas kernels: 0 us -> 152 us
  blocking collectives: 120 us -> 0 us
  matrix products: 61.3 us -> 0 us
  other arithmetic: 36.9 us -> 0.62 us
  local copies, waits for them, and re-layouts: 36.8 us -> 17.5 us
  starting transfers between devices: 16.5 us -> 0 us
  between operations: 16.7 us -> 0.69 us
    psum x2 -> x0, waiting for transfers between devices: 178 us -> none  [the longest x1 127 us: per_device(): lax.psum((grad_qkv, grad_qv, grad_out, grad_up, grad_up_bias, grad_down),...]
    pallas_call x0 -> x2, Pallas kernels: none -> 152 us  [the longest x1 149 us: per_device(): pl.pallas_call(layer_kernel, out_shape=[jax.ShapeDtypeStruct((B, 768), f3...]
    psum x2 -> x0, blocking collectives: 70.3 us -> none  [the longest x1 40.8 us: per_device(): lax.psum((grad_gain_one, grad_shift_one, grad_gain_two, grad_shift_two, g...]
    dot_general x25 -> x0, matrix products: 59.9 us -> none  [the longest x1 11.5 us: per_device(): lax.dot_general(cot_all, down_weight, contract_cols, preferred_element_ty...]
    unnamed x2 -> x0, blocking collectives: 49.3 us -> none
    unnamed x93 -> x15, local copies, waits for them, and re-layouts: 30.2 us -> 10 us
    reduce_sum x11 -> x0, other arithmetic: 16.4 us -> none  [the longest x2 5.81 us: layer_hat(): center = values - jnp.mean(values, axis=1, keepdims=True)]
    all_gather x2 -> x0, waiting for transfers between devices: 13.4 us -> none  [the longest x1 10.5 us: per_device(): cot_all = lax.all_gather(cotangent, 'mp', axis=0, tiled=True)]
  transfers between devices with their start and end apart: 7 -> 0, of which waited for: 4 -> 0; matrix products, arithmetic and copies ran while one was open for 13% -> 0% of each run, Pallas kernels for 0% -> 0%
where the time goes in v1:
time: 171 us
  Pallas kernels  152 us (89%)
  local copies, waits for them, and re-layouts  17.5 us (10%)
    pallas_call x1, Pallas kernels, per_device(): pl.pallas_call(layer_kernel, out_shape=[jax.ShapeDtypeStruct((B, 768), f3...  149 us
    unnamed x15, local copies, waits for them, and re-layouts  10 us
    another operation x9, local copies, waits for them, and re-layouts, per_device(): jnp.stack([gain_first, shift_first, out_bias, gain_second, shift_second,...  4.85 us

profile of v1, /device:TPU:0, one launch (start us, length us, event | category | flops | bytes accessed | tf_op | source)
XLA Modules:
  0.0 170.9 jit_solution(1756740060784498677)
XLA Ops:
  0.6 0.8 slice_reduce_fusion.1
  1.4 0.7 stack.27
  2.1 0.7 stack.28
  2.8 0.7 stack.29
  3.5 0.7 stack.30
  4.2 0.7 stack.31
  4.9 0.7 stack.32
  5.6 0.7 stack.33
  6.3 0.6 convert_element_type.7.vec_ref
  6.9 2.3 %copy.29.wqkv_ref = bf16[3,768,192]{2,1,0:T(8,128)(2,1)} copy(bf16[3,768,192]{1,2,0:T(8,128)(2,1)} %param.19) | data formatting | bytes 1769472 | tf_op args[4]
  9.2 148.8 %layer.1 = (f32[256,768]{1,0:T(8,128)}, f32[256,768]{1,0:T(8,128)}, f32[16,768]{1,0:T(8,128)}, bf16[2,768,384]{2,1,0:T(8,128)(2,1)}, bf16[2,768,384]{2,1,0:T(8,1...) custom-call(bf16[980,768]{1,0:T(8,128)(2,1)} %x_ref.1, s32[980]{0:T(1024)} %ids_ref.1, ...), custom_call_target="tpu_custom_call" | custom-call | tf_op jit(solution)/shard_map/layer/pallas_call | solution.py:668
  158.1 0.0 copy-start
  158.1 1.3 copy-done
  159.4 0.0 copy-start.1
  159.4 1.3 copy-done.1
  160.6 0.0 copy-start.2
  160.6 1.2 copy-done.2
  161.8 0.0 copy-start.3
  161.8 1.1 copy-done.3
  162.9 0.0 copy-start.4
  162.9 1.1 copy-done.4
  164.1 0.0 copy-start.5
  164.1 1.0 copy-done.5
  165.0 0.0 copy-start.6
  165.0 0.8 copy-done.6
  165.8 3.3 %finish.1 = (f32[245,768]{1,0:T(8,128)}, f32[245,768]{1,0:T(8,128)}, f32[768]{0:T(1024)}, f32[768]{0:T(1024)}, f32[3,768,192]{2,1,0:T(8,128)S(1)}, /*index=5*/f3...) custom-call(f32[256,768]{1,0:T(8,128)S(1)} %copy-done.3, ...), custom_call_target="tpu_custom_call" | custom-call | tf_op jit(solution)/shard_map/finish/pallas_call | solution.py:692
  169.1 1.8 %copy.30 = f32[3,768,192]{1,2,0:T(8,128)} copy(f32[3,768,192]{2,1,0:T(8,128)S(1)} %get-tuple-element.32) | data formatting | bytes 3538944 | tf_op jit(solution)/shard_map/finish/pallas_call | solution.py:692
  (3 shorter events, 0.1 us)
Async XLA Ops:
  158.1 1.3 copy-start
  159.4 1.3 copy-start.1
  160.6 1.2 copy-start.2
  161.8 1.1 copy-start.3
  162.9 1.1 copy-start.4
  164.1 1.0 copy-start.5
  165.0 0.8 copy-start.6

commit v2 on v1

--- a/solution.py
+++ b/solution.py
@@ -120,88 +120,231 @@
 
 
 class Reduce:
-    def __init__(self, spot, part, ybuf, zbuf, whole, send, recv):
-        self.zi, self.yi, self.ypeer, self.zpeers = spot
-        self.part, self.ybuf, self.zbuf, self.whole = part, ybuf, zbuf, whole
-        self.send, self.recv = send, recv
-        self.quarter = part.shape[1] // 4
-
-    def piece(self, ref, half, quarter):
-        return ref.at[half, pl.ds(pl.multiple_of(quarter * self.quarter, 16), self.quarter)]
-
-    def copy_y(self):
-        return remote(self.part.at[1 - self.yi], self.ybuf, self.send.at[0], self.recv.at[0], self.ypeer)
-
-    def copy_z(self, j):
-        src = self.piece(self.part, self.yi, self.zi ^ j)
-        return remote(src, self.zbuf.at[j - 1], self.send.at[j], self.recv.at[j], self.zpeers[j - 1])
-
-    def copy_back(self, j, quarter):
-        view = self.piece(self.whole, self.yi, quarter)
-        return remote(view, view, self.send.at[3 + j], self.recv.at[3 + j], self.zpeers[j - 1])
-
-    def copy_over(self, j, half):
-        view = self.piece(self.whole, half, self.zi ^ j)
-        return remote(view, view, self.send.at[7 + j], self.recv.at[7 + j], self.ypeer)
-
-    def one(self):
-        self.copy_y().start()
-
-    def two(self):
-        self.copy_y().wait_recv()
-
-        def add(q, carry):
-            span = pl.ds(pl.multiple_of(q * self.quarter, 16), self.quarter)
-            total = self.part[self.yi, span].astype(f32) + self.ybuf[span].astype(f32)
-            self.part[self.yi, span] = total.astype(bf16)
-            return carry
-
-        lax.fori_loop(0, 4, add, 0)
-        for j in (3, 2, 1):
-            self.copy_z(j).start()
-
-    def three(self):
-        span = pl.ds(pl.multiple_of(self.zi * self.quarter, 16), self.quarter)
-        total = self.part[self.yi, span].astype(f32)
-        for j in (1, 2, 3):
-            self.copy_z(j).wait_recv()
-            total = total + self.zbuf[j - 1].astype(f32)
-        self.whole[self.yi, span] = total.astype(bf16)
-        for j in (3, 2, 1):
-            self.copy_back(j, self.zi).start()
-        self.copy_over(0, self.yi).start()
-
-    def four(self):
-        for j in (1, 2, 3):
-            self.copy_back(j, self.zi ^ j).wait_recv()
-            self.copy_over(j, self.yi).start()
-
-    def five(self):
-        for j in range(4):
-            self.copy_over(j, 1 - self.yi).wait_recv()
+    def __init__(self, spot, first_y, refs):
+        self.zi, self.yi, self.over, self.above, self.below = spot
+        self.first_y = first_y
+        self.part, self.ybuf, self.up, self.down, self.whole, self.send, self.recv = refs
+        self.sent = []
+
+    def copy(self, src, dst, k, device):
+        return remote(src, dst, self.send.at[k], self.recv.at[k], device)
+
+    def begin(self, condition, make):
+        self.sent.append((condition, make))
+        if condition is None:
+            make().start()
+        else:
+            pl.when(condition())(lambda: make().start())
 
     def close(self):
-        self.copy_y().wait_send()
-        for j in (1, 2, 3):
-            self.copy_z(j).wait_send()
-            self.copy_back(j, self.zi).wait_send()
-        for j in range(4):
-            self.copy_over(j, self.yi).wait_send()
+        for condition, make in self.sent:
+            if condition is None:
+                make().wait_send()
+            else:
+                pl.when(condition())(lambda make=make: make().wait_send())
+
+    def chunks(self, first, count):
+        return self.part.at[self.yi if self.first_y else slice(None), pl.ds(first, count)]
+
+    def rising(self, first, count):
+        span = pl.ds(first - 1, count)
+        return self.up.at[span] if self.first_y else self.up.at[:, span]
+
+    def falling(self, first, count):
+        span = pl.ds(first, count)
+        return self.down.at[span] if self.first_y else self.down.at[:, span]
+
+    def result(self, chunk):
+        return self.whole.at[self.yi if self.first_y else slice(None), chunk]
+
+    def copy_up(self, first, count, src):
+        return self.copy(src, self.rising(first, count), 1, self.above)
+
+    def copy_down(self, first, count, src):
+        return self.copy(src, self.falling(first, count), 2, self.below)
+
+    def at(self, z):
+        return lambda: self.zi == z
+
+    def hop(self, n):
+        up_first, down_count = n, 4 - n
+
+        def up_view():
+            return self.chunks(n, 4 - n) if n == 1 else self.rising(n, 4 - n)
+
+        def down_view():
+            return self.chunks(0, 4 - n) if n == 1 else self.falling(0, 4 - n)
+
+        if n > 1:
+
+            @pl.when(self.zi == n - 1)
+            def _():
+                came = self.rising(n - 1, 5 - n)
+                self.copy_up(n - 1, 5 - n, came).wait_recv()
+                view, own = self.rising(n, 4 - n), self.chunks(n, 4 - n)
+                view[...] = (view[...].astype(f32) + own[...].astype(f32)).astype(bf16)
+
+            @pl.when(self.zi == 4 - n)
+            def _():
+                came = self.falling(0, 5 - n)
+                self.copy_down(0, 5 - n, came).wait_recv()
+                view, own = self.falling(0, 4 - n), self.chunks(0, 4 - n)
+                view[...] = (view[...].astype(f32) + own[...].astype(f32)).astype(bf16)
+
+        self.begin(self.at(n - 1), lambda: self.copy_up(up_first, 4 - n, up_view()))
+        self.begin(self.at(4 - n), lambda: self.copy_down(0, down_count, down_view()))
+
+    def total(self, store):
+        def plain(view):
+            return view[...].astype(f32)
+
+        @pl.when(self.zi == 0)
+        def _():
+            self.copy_down(0, 1, self.falling(0, 1)).wait_recv()
+            store(0, plain(self.chunks(0, 1)) + plain(self.falling(0, 1)))
+
+        @pl.when(self.zi == 3)
+        def _():
+            self.copy_up(3, 1, self.rising(3, 1)).wait_recv()
+            store(3, plain(self.chunks(3, 1)) + plain(self.rising(3, 1)))
+
+        for z in (1, 2):
+
+            @pl.when(self.zi == z)
+            def _(z=z):
+                value = plain(self.chunks(z, 1)) + plain(self.rising(z, 1)) + plain(self.falling(z, 1))
+                store(z, value)
+
+    def back(self, d):
+        for sign, base, ahead, room in ((-1, 3, self.above, lambda: self.zi < 3), (1, 6, self.below, lambda: self.zi > 0)):
+
+            def here(sign=sign):
+                return self.zi >= d if sign < 0 else self.zi <= 3 - d
+
+            def view(sign=sign):
+                return self.result(self.zi + sign * d)
+
+            if d > 0:
+
+                @pl.when(here())
+                def _():
+                    self.copy(view(), view(), base + d - 1, ahead).wait_recv()
+
+            if d < 3:
+                self.begin(
+                    lambda room=room, here=here: room() & here(),
+                    lambda view=view, base=base, ahead=ahead: self.copy(view(), view(), base + d, ahead),
+                )
+            if self.first_y and (d > 0 or sign < 0):
+                self.begin(
+                    here, lambda view=view, sign=sign: self.copy_over(self.yi, self.zi + sign * d)
+                )
+
+    def copy_over(self, half, chunk):
+        view = self.whole.at[half, chunk]
+        return self.copy(view, view, 9 + (chunk if self.first_y else 0), self.over)
+
+    def sum_over(self):
+        if self.first_y:
+            return self.copy(self.part.at[1 - self.yi], self.ybuf, 0, self.over)
+        return self.copy(self.part.at[1 - self.yi, self.zi], self.ybuf, 0, self.over)
+
+    def stage(self, k):
+        if self.first_y:
+            if k == 0:
+                self.begin(None, self.sum_over)
+            elif k == 1:
+                self.sum_over().wait_recv()
+
+                def add(c, carry):
+                    value = self.part[self.yi, c].astype(f32) + self.ybuf[c].astype(f32)
+                    self.part[self.yi, c] = value.astype(bf16)
+                    return carry
+
+                lax.fori_loop(0, 4, add, 0)
+                self.hop(1)
+            elif k in (2, 3):
+                self.hop(k)
+            elif k == 4:
+
+                def store(z, value):
+                    self.whole[self.yi, z] = value[0].astype(bf16)
+
+                self.total(store)
+                self.back(0)
+            elif k in (5, 6, 7):
+                self.back(k - 4)
+            else:
+                for c in range(4):
+                    self.copy_over(1 - self.yi, c).wait_recv()
+        else:
+            if k in (0, 1, 2):
+                self.hop(k + 1)
+            elif k == 3:
+
+                def store(z, value):
+                    self.part[:, z] = value[:, 0].astype(bf16)
+
+                self.total(store)
+                self.begin(None, self.sum_over)
+            elif k == 4:
+                self.sum_over().wait_recv()
+                value = self.part[self.yi, self.zi].astype(f32) + self.ybuf[...].astype(f32)
+                self.whole[self.yi, self.zi] = value.astype(bf16)
+                self.begin(None, lambda: self.copy_over(self.yi, self.zi))
+            elif k == 5:
+                self.copy_over(1 - self.yi, self.zi).wait_recv()
+                self.back(0)
+            else:
+                self.back(k - 5)
+
+
+FIRST_Y = (False, True, True, True, True, False, True, True, True, True)
+QUARTER = (64,) * 6 + (48,) * 4
+STAGES = 9
+
+POLLS = {
+    "down1": ((0, 0),),
+    "down2": ((1, 0),),
+    "up0": ((2, 0),),
+    "up1": ((3, 0),),
+    "up2": ((4, 0),),
+    "own": ((5, 0),),
+    "mlp2": ((1, 1),),
+    "mlp3": ((0, 1),),
+    "attend1": ((2, 1),),
+    "attend4": ((0, 2), (5, 1),),
+    "attend5": ((3, 1),),
+    "attend6": ((1, 2),),
+    "attend7": ((0, 3),),
+    "attend8": ((4, 1),),
+    "attend9": ((2, 2), (5, 2), (0, 4),),
+    "attend10": ((1, 3),),
+    "attend11": ((3, 2),),
+    "out": ((0, 5),),
+    "qkv0": ((2, 3), (5, 3), (6, 0),),
+    "qkv1": ((1, 4), (4, 2), (7, 0),),
+    "qkv2": ((8, 0),),
+    "first0": ((5, 4), (3, 3), (9, 0),),
+    "first2": ((0, 6), (2, 4),),
+    "first3": ((1, 5), (6, 1), (3, 4),),
+    "sums1": ((4, 3),),
+    "sums2": ((0, 7), (2, 5), (6, 2), (7, 1),),
+    "tail": ((1, 6), (3, 5), (5, 5), (4, 4), (0, 8), (6, 3), (7, 2), (8, 1), (2, 6), (1, 7), (9, 1), (3, 6), (5, 6), (4, 5), (8, 2), (7, 3), (6, 4), (2, 7), (9, 2), (3, 7), (5, 7), (8, 3), (1, 8), (4, 6), (7, 4), (6, 5), (9, 3), (2, 8), (5, 8), (3, 8), (8, 4), (4, 7), (7, 5), (6, 6), (9, 4), (8, 5), (4, 8), (7, 6), (6, 7), (9, 5), (8, 6), (7, 7), (9, 6), (6, 8), (8, 7), (9, 7), (7, 8), (8, 8), (9, 8),),
+}
 
 
 def layer_kernel(
-    x_ref, ids_ref, vec_ref, wqkv_ref, wo_ref, wup_ref, wdn_ref, cot_ref,
+    x_ref, ids_ref, gain_a, shift_a, bias_qv, bias_out, gain_b, shift_b, bias_up, bias_down,
+    wqkv_ref, wo_ref, wup_ref, wdn_ref, cot_ref,
     block_ref, input_ref, sums_ref, down_hbm, up_hbm, out_hbm, qkv_hbm,
     xp, stage, a1, keys, values, keys_t, values_t, qz_t, qz, kid, qid, probs, probs_last, rinv, ctx_t, ctx_all,
     wo_all, cot_all, a2, gate, du, do_all, dcz_t, dcz, delta, dq, dk, dv, dkb, dvb, own,
     rs_out, rs_both, rs_far, ms_out, ms_both, ms_far, m_own,
-    gd_part, gd_y, gd_z, gd_all, gu_part, gu_y, gu_z, gu_all,
-    go_part, go_y, go_z, go_all, gq_part, gq_y, gq_z, gq_all,
-    acc, v_mp, v_y, v_z,
+    vec_ref, acc, v_mp, v_y, v_z,
     wo_send, wo_recv, cot_send, cot_recv, ctx_send, ctx_recv, do_send, do_recv,
     rs_send, rs_recv, ms_send, ms_recv, rt_send, rt_recv,
-    gd_send, gd_recv, gu_send, gu_recv, go_send, go_recv, gq_send, gq_recv,
-    v_send, v_recv, local_sem,
+    v_send, v_recv, local_sem, block_refs,
 ):
     dp, me = lax.axis_index("dp"), lax.axis_index("mp")
     core, across, diagonal = (dp, me ^ 1), (dp, me ^ 2), (dp, me ^ 3)
@@ -209,7 +352,9 @@
     ypeer = (dp ^ 1, me)
     zpeers = [(dp ^ (2 * j), me) for j in (1, 2, 3)]
     place = (me, core, across)
-    spot = (zi, yi, ypeer, zpeers)
+    base = dp & ~7
+    above, below = (base + (((zi + 1) & 3) << 1) + yi, me), (base + (((zi + 3) & 3) << 1) + yi, me)
+    spot = (zi, yi, ypeer, above, below)
     share = cot_ref.shape[0]
 
     barrier = pltpu.get_barrier_semaphore()
@@ -219,6 +364,11 @@
 
     def vec(r, width=None):
         return vec_ref[r : r + 1, :] if width is None else vec_ref[r : r + 1, width[0] : width[1]]
+
+    for r, ref in enumerate((gain_a, shift_a, bias_out, gain_b, shift_b, bias_up, bias_down)):
+        vec_ref[r : r + 1, :] = ref[...].astype(f32).reshape(1, 768)
+    vec_ref[7:8, 0:192] = bias_qv[0:1, :].astype(f32)
+    vec_ref[7:8, 256:448] = bias_qv[1:2, :].astype(f32)
 
     stage[240:256, :] = jnp.zeros((16, 768), f32)
     stage[0:share, :] = cot_ref[...].astype(f32)
@@ -266,9 +416,9 @@
         hat, _ = layer_hat(xp[span, :].astype(f32))
         act = (hat * vec(0) + vec(1)).astype(bf16)
         a1[span, :] = act
-        q = (dot(act, wqkv_ref[0], NN) + vec(7, (0, 192))).astype(bf16)
-        k = dot(act, wqkv_ref[1], NN).astype(bf16)
-        v = (dot(act, wqkv_ref[2], NN) + vec(7, (256, 448))).astype(bf16)
+        q = (dot(act, wqkv_ref[0], NT) + vec(7, (0, 192))).astype(bf16)
+        k = dot(act, wqkv_ref[1], NT).astype(bf16)
+        v = (dot(act, wqkv_ref[2], NT) + vec(7, (256, 448))).astype(bf16)
         keys[span, :] = k
         values[span, :] = v
         keys_t[:, span] = k.T
@@ -401,24 +551,35 @@
 
     lax.fori_loop(0, 4, middle, 0)
 
-    def grad_tiles(part, left, right, width):
-        def tile(i, carry):
-            piece = dot(left[:, rows(i, width)], right[...], TN).astype(bf16)
-            part[0, rows(i, width), :] = piece[:, 0:384]
-            part[1, rows(i, width), :] = piece[:, 384:768]
-            return carry
-
-        lax.fori_loop(0, 768 // width, tile, 0)
-
-    reduce_down = Reduce(spot, gd_part, gd_y, gd_z, gd_all, gd_send, gd_recv)
-    reduce_up = Reduce(spot, gu_part, gu_y, gu_z, gu_all, gu_send, gu_recv)
-    reduce_out = Reduce(spot, go_part, go_y, go_z, go_all, go_send, go_recv)
-    reduce_qkv = Reduce(spot, gq_part, gq_y, gq_z, gq_all, gq_send, gq_recv)
-
-    grad_tiles(gd_part, gate, cot_all, B)
-    reduce_down.one()
-    grad_tiles(gu_part, a2, du, B)
-    reduce_up.one()
+    blocks = [Reduce(spot, first_y, refs) for first_y, refs in zip(FIRST_Y, block_refs)]
+    homes = [down_hbm.at[p] for p in range(3)] + [up_hbm.at[p] for p in range(3)]
+    homes += [out_hbm.at[0]] + [qkv_hbm.at[p] for p in range(3)]
+    saves = [pltpu.make_async_copy(blocks[p].whole, homes[p], local_sem.at[p]) for p in range(10)]
+
+    def poll(name):
+        for p, k in POLLS.get(name, ()):
+            blocks[p].stage(k)
+            if k == STAGES - 1:
+                saves[p].start()
+
+    def poll_at(prefix, index, count):
+        for n in range(count):
+            if POLLS.get(f"{prefix}{n}"):
+                pl.when(index == n)(lambda n=n: poll(f"{prefix}{n}"))
+
+    def stage_grad(p, piece):
+        quarter = QUARTER[p]
+        for h in range(2):
+            for c in range(4):
+                part = piece[c * quarter : (c + 1) * quarter, h * 384 : (h + 1) * 384]
+                blocks[p].part[h, c] = part.astype(bf16)
+
+    for t in range(3):
+        stage_grad(t, dot(gate[:, t * B : (t + 1) * B], cot_all[...], TN))
+        poll(f"down{t}")
+    for t in range(3):
+        stage_grad(3 + t, dot(a2[:, t * B : (t + 1) * B], du[...], TN))
+        poll(f"up{t}")
 
     grad_act = sum_in.finish()
     hat, factor = layer_hat(block_ref[...])
@@ -438,10 +599,11 @@
         s = me ^ (3 - i)
         m_own[...] = dot(gate[rows(s), :], wdn_ref[...], NN)
         sum_out.step(i, lambda: m_own[...])
+        poll_at("mlp", i, 4)
         return carry
 
+    poll("own")
     lax.fori_loop(0, 4, project_down, 0)
-    reduce_down.two()
 
     dk[...] = jnp.zeros(dk.shape, f32)
     dv[...] = jnp.zeros(dv.shape, f32)
@@ -467,12 +629,10 @@
         @pl.when(i == 2)
         def _():
             gather_do.forward()
-            reduce_up.two()
 
         @pl.when(i == 3)
         def _():
             gather_do.land_far()
-            reduce_down.three()
 
         grad_ctx = dot(wo_ref[...], do_all[span, :], NT).astype(bf16).astype(f32)
         for h in range(3):
@@ -489,27 +649,34 @@
         @pl.when(s != 3)
         def _():
             dv[0:TOP, :] += dot(probs[s], dcz[...], NN)
-            ref = probs.at[s]
-
-            def head(h, inner):
-                grad = back_head(s, h, 0, TOP, 0, B, ref)
-                stage[pl.ds(pl.multiple_of(h * HD, HD), HD), 0:B] = grad
-                return inner
-
-            lax.fori_loop(0, 3, head, 0)
-            dk[0:TOP, :] += dot(probs[s], qz[s], NN)
 
         @pl.when(s == 3)
         def _():
             dv[...] += dot(probs_last[...], dcz[...], NN)
 
-            def head(h, inner):
-                here = pl.ds(pl.multiple_of(h * HD, HD), HD)
+        def head(h, inner):
+            here = pl.ds(pl.multiple_of(h * HD, HD), HD)
+
+            @pl.when(s != 3)
+            def _():
+                stage[here, 0:B] = back_head(s, h, 0, TOP, 0, B, probs.at[s])
+
+            @pl.when(s == 3)
+            def _():
                 stage[here, 0:128] = back_head(s, h, 0, 1024, 0, 128, probs_last)
                 stage[here, 128:256] = back_head(s, h, 768, 1024, 128, 256, probs_last)
-                return inner
-
-            lax.fori_loop(0, 3, head, 0)
+
+            poll_at("attend", i * 3 + h, 12)
+            return inner
+
+        lax.fori_loop(0, 3, head, 0)
+
+        @pl.when(s != 3)
+        def _():
+            dk[0:TOP, :] += dot(probs[s], qz[s], NN)
+
+        @pl.when(s == 3)
+        def _():
             dk[...] += dot(probs_last[...], qz[s], NN)
 
         dq[span, :] = (stage[0:192, 0:B] * HD**-0.5).T.astype(bf16)
@@ -518,19 +685,13 @@
     dcz_t[...] = jnp.zeros(dcz_t.shape, bf16)
     lax.fori_loop(0, 4, back_block, 0)
 
-    grad_out = dot(ctx_t[...], do_all[...], NN).astype(bf16)
-    go_part[0] = grad_out[:, 0:384]
-    go_part[1] = grad_out[:, 384:768]
-    reduce_out.one()
-    reduce_up.three()
-
+    stage_grad(6, dot(ctx_t[...], do_all[...], NN))
+    poll("out")
     dkb[...] = dk[...].astype(bf16)
     dvb[...] = dv[...].astype(bf16)
     for t, ref in enumerate((dq, dkb, dvb)):
-        piece = dot(ref[...], a1[...], TN).astype(bf16)
-        gq_part[0, t * 192 : (t + 1) * 192, :] = piece[:, 0:384]
-        gq_part[1, t * 192 : (t + 1) * 192, :] = piece[:, 384:768]
-    reduce_qkv.one()
+        stage_grad(7 + t, dot(ref[...], a1[...], TN))
+        poll(f"qkv{t}")
     acc[9:10, 0:192] = column_sum(dq[...].astype(f32))
     acc[9:10, 256:448] = column_sum(dvb[...].astype(f32))
 
@@ -539,14 +700,15 @@
     def project_back(i, carry):
         s = me ^ (3 - i)
         span = rows(s)
-        grad = dot(dq[span, :], wqkv_ref[0], NT)
-        grad = grad + dot(dkb[span, :], wqkv_ref[1], NT)
-        grad = grad + dot(dvb[span, :], wqkv_ref[2], NT)
+        grad = dot(dq[span, :], wqkv_ref[0], NN)
+        grad = grad + dot(dkb[span, :], wqkv_ref[1], NN)
+        grad = grad + dot(dvb[span, :], wqkv_ref[2], NN)
         hat, _ = layer_hat(xp[span, :].astype(f32))
         acc[0:1, :] += column_sum(grad * hat)
         acc[1:2, :] += column_sum(grad)
         own[...] = grad
         sum_first.step(i, lambda: own[...])
+        poll_at("first", i, 4)
         return carry
 
     lax.fori_loop(0, 4, project_back, 0)
@@ -556,32 +718,22 @@
     v_lands = [remote(v_mp.at[me ^ j], v_mp.at[me ^ j], v_send.at[j - 1], v_recv.at[j - 1], (dp, me ^ j)) for j in (1, 2, 3)]
     for copy in v_copies:
         copy.start()
-    reduce_out.two()
-    reduce_qkv.two()
+    poll("sums0")
     for copy in v_lands:
         copy.wait_recv()
     acc[0:8, :] = v_mp[0, 0:8, :] + v_mp[1, 0:8, :] + v_mp[2, 0:8, :] + v_mp[3, 0:8, :]
     vy_copy = remote(acc, v_y, v_send.at[3], v_recv.at[3], ypeer)
     vy_copy.start()
-    reduce_down.four()
-    reduce_up.four()
-    reduce_out.three()
+    poll("sums1")
     vy_copy.wait_recv()
     v_z[zi] = acc[...] + v_y[...]
     vz_copies = [remote(v_z.at[zi], v_z.at[zi], v_send.at[3 + j], v_recv.at[3 + j], zpeers[j - 1]) for j in (1, 2, 3)]
     vz_lands = [remote(v_z.at[zi ^ j], v_z.at[zi ^ j], v_send.at[3 + j], v_recv.at[3 + j], zpeers[j - 1]) for j in (1, 2, 3)]
     for copy in vz_copies:
         copy.start()
-    reduce_qkv.three()
+    poll("sums2")
 
     block_ref[...] = block_ref[...] + (sum_out.finish() + vec(6))
-    reduce_down.five()
-    save_down = pltpu.make_async_copy(gd_all, down_hbm, local_sem.at[0])
-    save_down.start()
-    reduce_up.five()
-    save_up = pltpu.make_async_copy(gu_all, up_hbm, local_sem.at[1])
-    save_up.start()
-    reduce_out.four()
     for copy in vz_lands:
         copy.wait_recv()
     sums_ref[...] = v_z[0] + v_z[1] + v_z[2] + v_z[3]
@@ -590,62 +742,99 @@
     hat, factor = layer_hat(xp[rows(me), :].astype(f32))
     input_ref[...] = input_ref[...] + layer_back(grad_act * vec(0), hat, factor)
 
-    reduce_out.five()
-    save_out = pltpu.make_async_copy(go_all, out_hbm, local_sem.at[2])
-    save_out.start()
-    reduce_qkv.four()
-    reduce_qkv.five()
-    save_qkv = pltpu.make_async_copy(gq_all, qkv_hbm, local_sem.at[3])
-    save_qkv.start()
+    poll("tail")
 
     for copy in v_copies + [vy_copy] + vz_copies:
         copy.wait_send()
     for gather in [gather_wo, gather_cot, gather_do] + [gather_ctx(s) for s in range(4)]:
         gather.close()
-    for reduce in (reduce_down, reduce_up, reduce_out, reduce_qkv):
-        reduce.close()
-    for save in (save_down, save_up, save_out, save_qkv):
+    for block in blocks:
+        block.close()
+    for save in saves:
         save.wait()
 
 
 def finish_kernel(
-    block_ref, input_ref, sums_ref, down_ref, up_ref, out_ref, qkv_ref,
+    block_hbm, input_hbm, sums_hbm, down_hbm, up_hbm, out_hbm, qkv_hbm,
     block_out, input_grad, gain_first, shift_first, grad_qkv, grad_qv, grad_out, out_bias, gain_second, shift_second,
     grad_up, up_bias, grad_down, down_bias,
+    block_v, input_v, sums, down_v, up_v, out_v, qkv_v, block_w, input_w, down_w, up_w, out_w, qkv_w,
+    in_sem, out_sem,
 ):
     share = block_out.shape[0]
-    block_out[...] = block_ref[0:share, :]
-    input_grad[...] = input_ref[0:share, :]
+    pairs = (
+        (down_hbm, down_v), (up_hbm, up_v), (qkv_hbm, qkv_v), (block_hbm, block_v), (input_hbm, input_v),
+        (out_hbm, out_v), (sums_hbm, sums),
+    )
+    loads = [pltpu.make_async_copy(src, dst, in_sem.at[k]) for k, (src, dst) in enumerate(pairs)]
+    for load in loads:
+        load.start()
+    stores = []
+
+    def save(src, dst):
+        stores.append(pltpu.make_async_copy(src, dst, out_sem.at[len(stores)]))
+        stores[-1].start()
+
+    def widen(source, p, put):
+        quarter = source.shape[3]
+        for h in range(2):
+            for c in range(4):
+                put(slice(c * quarter, (c + 1) * quarter), slice(h * 384, (h + 1) * 384), source[p, h, c].astype(f32))
+
+    for k, (source, wide, target) in enumerate(((down_v, down_w, grad_down), (up_v, up_w, grad_up))):
+        loads[k].wait()
+        for p in range(3):
+
+            def put(r, lanes, value):
+                wide[p * B + r.start : p * B + r.stop, lanes] = value
+
+            widen(source, p, put)
+        save(wide, target)
+    loads[2].wait()
+    for p in range(3):
+
+        def put(r, lanes, value):
+            qkv_w[p, r, lanes] = value
+
+        widen(qkv_v, p, put)
+    save(qkv_w, grad_qkv)
+    for k, source, wide, target in ((3, block_v, block_w, block_out), (4, input_v, input_w, input_grad)):
+        loads[k].wait()
+        wide[...] = source[0:share, :]
+        save(wide, target)
+    loads[5].wait()
+
+    def put(r, lanes, value):
+        out_w[r, lanes] = value
+
+    widen(out_v, 0, put)
+    save(out_w, grad_out)
+    loads[6].wait()
     for r, ref in enumerate((gain_first, shift_first, gain_second, shift_second, out_bias, down_bias)):
-        ref[...] = sums_ref[r, :]
-    up_bias[...] = sums_ref[8, :]
-    grad_qv[0:1, :] = sums_ref[9:10, 0:192]
-    grad_qv[1:2, :] = sums_ref[9:10, 256:448]
-    for source, target in ((down_ref, grad_down), (up_ref, grad_up), (out_ref, grad_out)):
-        for half in range(2):
-            target[:, half * 384 : (half + 1) * 384] = source[half].astype(f32)
-    for t in range(3):
-        for half in range(2):
-            turned = qkv_ref[half, t * 192 : (t + 1) * 192, :].astype(f32).T
-            grad_qkv[t, half * 384 : (half + 1) * 384, :] = turned
+        ref[...] = sums[r, :]
+    up_bias[...] = sums[8, :]
+    grad_qv[0:1, :] = sums[9:10, 0:192]
+    grad_qv[1:2, :] = sums[9:10, 256:448]
+    for store in stores:
+        store.wait()
 
 
 def per_device(
     inputs, image_of_row, gain_first, shift_first, qkv_weight, qv_bias, out_weight, out_bias, gain_second,
     shift_second, up_weight, up_bias, down_weight, down_bias, cotangent,
 ):
-    qv_row = jnp.concatenate([jnp.pad(qv_bias[0], (0, 64)), jnp.pad(qv_bias[1], (0, 320))])
-    packed = jnp.stack(
-        [gain_first, shift_first, out_bias, gain_second, shift_second, up_bias, down_bias, qv_row]
-    ).astype(f32)
     share = cotangent.shape[0]
     vmem, smem, anyspace = (pl.BlockSpec(memory_space=m) for m in (pltpu.VMEM, pltpu.SMEM, pl.ANY))
 
     def shape(*dims, dtype=bf16):
         return pltpu.VMEM(dims, dtype)
 
-    def job(n):
-        return [shape(2, n, 384), shape(n, 384), shape(3, n // 4, 384), shape(2, n, 384)]
+    dma = pltpu.SemaphoreType.DMA
+
+    def block_scratch(first_y, r):
+        over = shape(4, r, 384) if first_y else shape(r, 384)
+        along = shape(3, r, 384) if first_y else shape(2, 3, r, 384)
+        return [shape(2, 4, r, 384), over, along, along, shape(2, 4, r, 384), dma((13,)), dma((13,))]
 
     scratch = [
         shape(1024, 768), shape(272, 768, dtype=f32), shape(1024, 768),
@@ -660,47 +849,52 @@
         shape(1024, 192), shape(1024, 192), shape(B, 768, dtype=f32),
         shape(3, B, 768), shape(2, B, 768), shape(B, 768),
         shape(3, B, 768), shape(2, B, 768), shape(B, 768), shape(B, 768, dtype=f32),
-        *job(768), *job(768), *job(192), *job(576),
+        shape(8, 768, dtype=f32),
         shape(16, 768, dtype=f32), shape(4, 16, 768, dtype=f32), shape(16, 768, dtype=f32), shape(4, 16, 768, dtype=f32),
     ]
-    dma = pltpu.SemaphoreType.DMA
-    scratch += [dma((3,))] * 4 + [dma((4, 3))] * 2 + [dma((3,))] * 8 + [dma((11,))] * 8 + [dma((7,))] * 2 + [dma((4,))]
+    scratch += [dma((3,))] * 4 + [dma((4, 3))] * 2 + [dma((3,))] * 8 + [dma((7,))] * 2 + [dma((10,))]
+    scratch += [[block_scratch(first_y, r) for first_y, r in zip(FIRST_Y, QUARTER)]]
     results = pl.pallas_call(
         layer_kernel,
         out_shape=[
             jax.ShapeDtypeStruct((B, 768), f32),
             jax.ShapeDtypeStruct((B, 768), f32),
             jax.ShapeDtypeStruct((16, 768), f32),
-            jax.ShapeDtypeStruct((2, 768, 384), bf16),
-            jax.ShapeDtypeStruct((2, 768, 384), bf16),
-            jax.ShapeDtypeStruct((2, 192, 384), bf16),
-            jax.ShapeDtypeStruct((2, 576, 384), bf16),
+            jax.ShapeDtypeStruct((3, 2, 4, 64, 384), bf16),
+            jax.ShapeDtypeStruct((3, 2, 4, 64, 384), bf16),
+            jax.ShapeDtypeStruct((1, 2, 4, 48, 384), bf16),
+            jax.ShapeDtypeStruct((3, 2, 4, 48, 384), bf16),
         ],
-        in_specs=[vmem, smem] + [vmem] * 6,
+        in_specs=[vmem, smem] + [vmem] * 13,
         out_specs=[vmem] * 3 + [anyspace] * 4,
         scratch_shapes=scratch,
         compiler_params=pltpu.CompilerParams(
             collective_id=0, has_side_effects=True, vmem_limit_bytes=60 * 2**20
         ),
         name="layer",
-    )(inputs, image_of_row, packed, qkv_weight, out_weight, up_weight, down_weight, cotangent)
+    )(
+        inputs, image_of_row, gain_first, shift_first, qv_bias, out_bias, gain_second, shift_second, up_bias, down_bias,
+        jnp.swapaxes(qkv_weight, 1, 2), out_weight, up_weight, down_weight, cotangent,
+    )
 
     def out(*dims):
         return jax.ShapeDtypeStruct(dims, f32)
 
-    return tuple(
-        pl.pallas_call(
-            finish_kernel,
-            out_shape=[
-                out(share, 768), out(share, 768), out(768), out(768), out(3, 768, 192), out(2, 192), out(192, 768),
-                out(768), out(768), out(768), out(768, 768), out(768), out(768, 768), out(768),
-            ],
-            in_specs=[vmem] * 7,
-            out_specs=[vmem] * 14,
-            compiler_params=pltpu.CompilerParams(vmem_limit_bytes=32 * 2**20),
-            name="finish",
-        )(*results)
-    )
+    wide = [shape(share, 768, dtype=f32)] * 2 + [shape(768, 768, dtype=f32)] * 2
+    outputs = pl.pallas_call(
+        finish_kernel,
+        out_shape=[
+            out(share, 768), out(share, 768), out(768), out(768), out(3, 192, 768), out(2, 192), out(192, 768),
+            out(768), out(768), out(768), out(768, 768), out(768), out(768, 768), out(768),
+        ],
+        in_specs=[anyspace] * 7,
+        out_specs=[anyspace if k in (0, 1, 4, 6, 10, 12) else vmem for k in range(14)],
+        scratch_shapes=[pltpu.VMEM(r.shape, r.dtype) for r in results]
+        + wide + [shape(192, 768, dtype=f32), shape(3, 192, 768, dtype=f32), dma((7,)), dma((6,))],
+        compiler_params=pltpu.CompilerParams(vmem_limit_bytes=60 * 2**20),
+        name="finish",
+    )(*results)
+    return (*outputs[:4], jnp.swapaxes(outputs[4], 1, 2), *outputs[5:])
 
 
 def solution(mesh):

time: 171 us -> 143 us (0.84)
  local copies, waits for them, and re-layouts: 17.5 us -> 0 us
  Pallas kernels: 152 us -> 142 us
    pallas_call x1, Pallas kernels: 149 us -> 137 us  [per_device(): pl.pallas_call(layer_kernel, out_shape=[jax.ShapeDtypeStruct((B, 768), f3...]
    unnamed x15 -> x0, local copies, waits for them, and re-layouts: 10 us -> none
    another operation x9 -> x0, local copies, waits for them, and re-layouts: 4.85 us -> none  [per_device(): jnp.stack([gain_first, shift_first, out_bias, gain_second, shift_second,...]
    pallas_call x1, Pallas kernels: 3.26 us -> 5.51 us  [per_device(): pl.pallas_call(finish_kernel, out_shape=[out(share, 768), out(share, 768)...]
    pallas_call x1 -> x0, local copies, waits for them, and re-layouts: 1.8 us -> none  [per_device(): pl.pallas_call(finish_kernel, out_shape=[out(share, 768), out(share, 768)...]
where the time goes in v2:
time: 143 us
  Pallas kernels  142 us (99%)
    pallas_call x1, Pallas kernels, per_device(): pl.pallas_call(layer_kernel, out_shape=[jax.ShapeDtypeStruct((B, 768), f3...  137 us
    pallas_call x1, Pallas kernels, per_device(): pl.pallas_call(finish_kernel, out_shape=[out(share, 768), out(share, 768)...  5.51 us

profile of v2, /device:TPU:0, one launch (start us, length us, event | category | flops | bytes accessed | tf_op | source)
XLA Modules:
  0.0 143.0 jit_solution(4494573301334148132)
XLA Ops:
  0.7 136.7 %layer.1 = (f32[256,768]{1,0:T(8,128)}, f32[256,768]{1,0:T(8,128)}, f32[16,768]{1,0:T(8,128)}, bf16[3,2,4,64,384]{4,3,2,1,0:T(8,128)(2,1)}, bf16[3,2,4,64,384]{4...) custom-call(bf16[980,768]{1,0:T(8,128)(2,1)} %x_ref.1, s32[980]{0:T(1024)} %ids_ref.1, ...), custom_call_target="tpu_custom_call" | custom-call | tf_op jit(solution)/shard_map/layer/pallas_call | solution.py:857
  137.4 5.5 %finish.1 = (f32[245,768]{1,0:T(8,128)}, f32[245,768]{1,0:T(8,128)}, f32[768]{0:T(1024)}, f32[768]{0:T(1024)}, f32[3,192,768]{2,1,0:T(8,128)}, /*index=5*/f32[2,...) custom-call(f32[256,768]{1,0:T(8,128)} %get-tuple-element.35.block_h, ...), custom_call_target="tpu_custom_call" | custom-call | tf_op jit(solution)/shard_map/finish/pallas_call | solution.py:884

commit v3 on v2

--- a/solution.py
+++ b/solution.py
@@ -89,7 +89,7 @@
         dst = self.far if k == 1 else self.both.at[k // 2]
         return remote(src, dst, self.send.at[k], self.recv.at[k], self.across if k == 1 else self.core)
 
-    def step(self, i, value):
+    def step(self, i, value, hold=False):
         @pl.when(i == 0)
         def _():
             self.out[0] = value().astype(bf16)
@@ -97,9 +97,12 @@
 
         @pl.when(i == 1)
         def _():
-            self.copy(0).wait_recv()
-            self.out[1] = (value() + self.both[0].astype(f32)).astype(bf16)
-            self.copy(1).start()
+            if hold:
+                self.out[1] = value().astype(bf16)
+            else:
+                self.copy(0).wait_recv()
+                self.out[1] = (value() + self.both[0].astype(f32)).astype(bf16)
+                self.copy(1).start()
 
         @pl.when(i == 2)
         def _():
@@ -109,6 +112,11 @@
         @pl.when(i == 3)
         def _():
             self.own[...] = value()
+
+    def release(self):
+        self.copy(0).wait_recv()
+        self.out[1] = (self.out[1].astype(f32) + self.both[0].astype(f32)).astype(bf16)
+        self.copy(1).start()
 
     def finish(self):
         self.copy(2).wait_recv()
@@ -299,44 +307,41 @@
                 self.back(k - 5)
 
 
-FIRST_Y = (False, True, True, True, True, False, True, True, True, True)
+FIRST_Y = (False, True, True, True, True, True, True, True, True, True)
 QUARTER = (64,) * 6 + (48,) * 4
 STAGES = 9
 
 POLLS = {
-    "down1": ((0, 0),),
-    "down2": ((1, 0),),
-    "up0": ((2, 0),),
-    "up1": ((3, 0),),
-    "up2": ((4, 0),),
-    "own": ((5, 0),),
-    "mlp2": ((1, 1),),
-    "mlp3": ((0, 1),),
-    "attend1": ((2, 1),),
-    "attend4": ((0, 2), (5, 1),),
-    "attend5": ((3, 1),),
-    "attend6": ((1, 2),),
-    "attend7": ((0, 3),),
-    "attend8": ((4, 1),),
-    "attend9": ((2, 2), (5, 2), (0, 4),),
-    "attend10": ((1, 3),),
-    "attend11": ((3, 2),),
-    "out": ((0, 5),),
-    "qkv0": ((2, 3), (5, 3), (6, 0),),
-    "qkv1": ((1, 4), (4, 2), (7, 0),),
-    "qkv2": ((8, 0),),
-    "first0": ((5, 4), (3, 3), (9, 0),),
-    "first2": ((0, 6), (2, 4),),
-    "first3": ((1, 5), (6, 1), (3, 4),),
-    "sums1": ((4, 3),),
-    "sums2": ((0, 7), (2, 5), (6, 2), (7, 1),),
-    "tail": ((1, 6), (3, 5), (5, 5), (4, 4), (0, 8), (6, 3), (7, 2), (8, 1), (2, 6), (1, 7), (9, 1), (3, 6), (5, 6), (4, 5), (8, 2), (7, 3), (6, 4), (2, 7), (9, 2), (3, 7), (5, 7), (8, 3), (1, 8), (4, 6), (7, 4), (6, 5), (9, 3), (2, 8), (5, 8), (3, 8), (8, 4), (4, 7), (7, 5), (6, 6), (9, 4), (8, 5), (4, 8), (7, 6), (6, 7), (9, 5), (8, 6), (7, 7), (9, 6), (6, 8), (8, 7), (9, 7), (7, 8), (8, 8), (9, 8),),
+    "down0": ((0, 0),),
+    "down1": ((1, 0),),
+    "down2": ((2, 0),),
+    "up0": ((3, 0), (1, 1),),
+    "up1": ((4, 0),),
+    "up2": ((0, 1), (5, 0),),
+    "rs1": ((2, 1), (1, 2),),
+    "own": ((0, 2), (3, 1),),
+    "attend0": ((1, 3), (2, 2),),
+    "attend3": ((1, 4), (0, 3), (3, 2),),
+    "attend4": ((2, 3), (4, 1),),
+    "do": ((5, 1), (1, 5),),
+    "attend6": ((0, 4), (2, 4), (3, 3),),
+    "attend7": ((1, 6), (4, 2),),
+    "attend9": ((0, 5), (3, 4), (5, 2),),
+    "attend10": ((1, 7), (2, 5), (4, 3),),
+    "out": ((6, 0),),
+    "qkv0": ((7, 0),),
+    "qkv1": ((1, 8), (0, 6), (8, 0),),
+    "qkv2": ((9, 0),),
+    "first0": ((3, 5),),
+    "first2": ((4, 4), (5, 3),),
+    "first3": ((2, 6), (6, 1),),
+    "tail": ((10, 0), (11, 0), (0, 7), (3, 6), (7, 1), (4, 5), (5, 4), (6, 2), (2, 7), (8, 1), (0, 8), (7, 2), (3, 7), (12, 0), (4, 6), (6, 3), (9, 1), (10, 1), (5, 5), (8, 2), (7, 3), (4, 7), (6, 4), (9, 2), (5, 6), (8, 3), (7, 4), (6, 5), (2, 8), (5, 7), (9, 3), (3, 8), (8, 4), (7, 5), (6, 6), (10, 2), (9, 4), (8, 5), (4, 8), (7, 6), (6, 7), (5, 8), (10, 3), (9, 5), (7, 7), (8, 6), (6, 8), (9, 6), (8, 7), (7, 8), (9, 7), (8, 8), (9, 8),),
 }
 
 
 def layer_kernel(
-    x_ref, ids_ref, gain_a, shift_a, bias_qv, bias_out, gain_b, shift_b, bias_up, bias_down,
-    wqkv_ref, wo_ref, wup_ref, wdn_ref, cot_ref,
+    x_hbm, ids_ref, gain_a, shift_a, bias_qv, bias_out, gain_b, shift_b, bias_up, bias_down,
+    wqkv_hbm, wo_hbm, wup_hbm, wdn_hbm, cot_hbm,
     block_ref, input_ref, sums_ref, down_hbm, up_hbm, out_hbm, qkv_hbm,
     xp, stage, a1, keys, values, keys_t, values_t, qz_t, qz, kid, qid, probs, probs_last, rinv, ctx_t, ctx_all,
     wo_all, cot_all, a2, gate, du, do_all, dcz_t, dcz, delta, dq, dk, dv, dkb, dvb, own,
@@ -344,7 +349,7 @@
     vec_ref, acc, v_mp, v_y, v_z,
     wo_send, wo_recv, cot_send, cot_recv, ctx_send, ctx_recv, do_send, do_recv,
     rs_send, rs_recv, ms_send, ms_recv, rt_send, rt_recv,
-    v_send, v_recv, local_sem, block_refs,
+    v_send, v_recv, local_sem, load_sem, x_ref, wqkv_ref, wup_ref, wdn_ref, cot_ref, vec_raw, qv_raw, block_refs,
 ):
     dp, me = lax.axis_index("dp"), lax.axis_index("mp")
     core, across, diagonal = (dp, me ^ 1), (dp, me ^ 2), (dp, me ^ 3)
@@ -355,7 +360,7 @@
     base = dp & ~7
     above, below = (base + (((zi + 1) & 3) << 1) + yi, me), (base + (((zi + 3) & 3) << 1) + yi, me)
     spot = (zi, yi, ypeer, above, below)
-    share = cot_ref.shape[0]
+    share = cot_hbm.shape[0]
 
     barrier = pltpu.get_barrier_semaphore()
     partners = [core, across, diagonal, ypeer] + zpeers
@@ -365,22 +370,39 @@
     def vec(r, width=None):
         return vec_ref[r : r + 1, :] if width is None else vec_ref[r : r + 1, width[0] : width[1]]
 
-    for r, ref in enumerate((gain_a, shift_a, bias_out, gain_b, shift_b, bias_up, bias_down)):
-        vec_ref[r : r + 1, :] = ref[...].astype(f32).reshape(1, 768)
-    vec_ref[7:8, 0:192] = bias_qv[0:1, :].astype(f32)
-    vec_ref[7:8, 256:448] = bias_qv[1:2, :].astype(f32)
-
+    pairs = [(cot_hbm, cot_ref), (x_hbm, x_ref), (wo_hbm, wo_all.at[me]), (bias_qv, qv_raw)]
+    pairs += list(zip((gain_a, shift_a, bias_out, gain_b, shift_b, bias_up, bias_down), vec_raw))
+    pairs += [(wqkv_hbm, wqkv_ref), (wup_hbm, wup_ref), (wdn_hbm, wdn_ref)]
+    loads = [pltpu.make_async_copy(src, dst, load_sem.at[k]) for k, (src, dst) in enumerate(pairs)]
+    for load in loads:
+        load.start()
+    pl.semaphore_wait(barrier, len(partners))
+
+    gather_wo = Gather(place, lambda s: wo_all.at[s], lambda k: wo_send.at[k], lambda k: wo_recv.at[k])
+    loads[2].wait()
+    gather_wo.start()
+
+    def gather_cot(q):
+        return Gather(
+            place,
+            lambda s: cot_all.at[pl.ds(pl.multiple_of(s * B + q * 64, 64), 64)],
+            lambda k: cot_send.at[q, k],
+            lambda k: cot_recv.at[q, k],
+        )
+
+    loads[0].wait()
     stage[240:256, :] = jnp.zeros((16, 768), f32)
     stage[0:share, :] = cot_ref[...].astype(f32)
     cot_all[rows(me), :] = stage[0:B, :].astype(bf16)
-    wo_all[me] = wo_ref[...]
+    gather_cot(0).start()
     acc[...] = jnp.zeros(acc.shape, f32)
-    pl.semaphore_wait(barrier, len(partners))
-
-    gather_wo = Gather(place, lambda s: wo_all.at[s], lambda k: wo_send.at[k], lambda k: wo_recv.at[k])
-    gather_cot = Gather(place, lambda s: cot_all.at[rows(s)], lambda k: cot_send.at[k], lambda k: cot_recv.at[k])
-    gather_wo.start()
-    gather_cot.start()
+    for k in range(3, 11):
+        loads[k].wait()
+    for r, ref in enumerate(vec_raw):
+        vec_ref[r : r + 1, :] = ref[...].astype(f32).reshape(1, 768)
+    vec_ref[7:8, 0:192] = qv_raw[0:1, :].astype(f32)
+    vec_ref[7:8, 256:448] = qv_raw[1:2, :].astype(f32)
+    loads[1].wait()
 
     row_in = lax.broadcasted_iota(i32, (B, 768), 0)
     for s in range(4):
@@ -430,6 +452,7 @@
             qz[s, h * B : (h + 1) * B, :] = jnp.where(lane_head == h, q, 0.0).astype(bf16)
         return carry
 
+    loads[11].wait()
     lax.fori_loop(0, 4, project, 0)
 
     def gather_ctx(s):
@@ -475,10 +498,6 @@
         def _():
             gather_wo.forward()
 
-        @pl.when(s == 2)
-        def _():
-            gather_cot.forward()
-
         return carry
 
     lax.fori_loop(0, 3, attend_top, 0)
@@ -500,14 +519,15 @@
     lax.fori_loop(0, 3, attend_last, 0)
     send_ctx(3)
 
+    for q in (1, 2, 3):
+        gather_cot(q).start()
     gather_wo.land_core()
     gather_wo.land_far()
-    gather_cot.land_core()
-    gather_cot.land_far()
     for s in range(4):
         gather_ctx(s).forward()
-
-    sum_in = Scatter(place, rs_out, rs_both, rs_far, own, rs_send, rs_recv)
+    loads[12].wait()
+    loads[13].wait()
+
     zeros_w = jnp.zeros((HD, 768), bf16)
 
     def middle(i, carry):
@@ -532,32 +552,75 @@
             block_ref[...] = h
 
         hat, _ = layer_hat(h)
-        stage[0:B, :] = hat
         act = (hat * vec(3) + vec(4)).astype(bf16)
         a2[span, :] = act
         u = dot(act, wup_ref[...], NN) + vec(5)
         cdf = 0.5 * (1.0 + lax.erf(u * 0.7071067811865476))
         gate[span, :] = (u * cdf).astype(bf16)
-        slope = cdf + u * (0.3989422804014327 * jnp.exp(-0.5 * (u * u)))
-        grad_u = (dot(cot_all[span, :], wdn_ref[...], NT) * slope).astype(bf16)
-        du[span, :] = grad_u
-        acc[8:9, :] += column_sum(grad_u.astype(f32))
-        grad_act = dot(grad_u, wup_ref[...], NT)
-        acc[2:3, :] += column_sum(grad_act * stage[0:B, :])
-        acc[3:4, :] += column_sum(grad_act)
-        own[...] = grad_act
-        sum_in.step(i, lambda: own[...])
+        du[span, :] = (cdf + u * (0.3989422804014327 * jnp.exp(-0.5 * (u * u)))).astype(bf16)
         return carry
 
     lax.fori_loop(0, 4, middle, 0)
+
+    for q in range(4):
+        gather_cot(q).forward()
+    for q in range(4):
+        gather_cot(q).land_core()
+        gather_cot(q).land_far()
 
     blocks = [Reduce(spot, first_y, refs) for first_y, refs in zip(FIRST_Y, block_refs)]
     homes = [down_hbm.at[p] for p in range(3)] + [up_hbm.at[p] for p in range(3)]
     homes += [out_hbm.at[0]] + [qkv_hbm.at[p] for p in range(3)]
     saves = [pltpu.make_async_copy(blocks[p].whole, homes[p], local_sem.at[p]) for p in range(10)]
 
+    def sum_copy(slot, k, device, ref=v_mp):
+        view = ref.at[slot]
+        return remote(view, view, v_send.at[k], v_recv.at[k], device)
+
+    def sum_y():
+        return remote(acc, v_y, v_send.at[3], v_recv.at[3], ypeer)
+
+    def sums(k):
+        if k == 0:
+            v_mp[me] = acc[...]
+            for j in (1, 2, 3):
+                sum_copy(me, j - 1, (dp, me ^ j)).start()
+        elif k == 1:
+            for j in (1, 2, 3):
+                sum_copy(me ^ j, j - 1, (dp, me ^ j)).wait_recv()
+                sum_copy(me, j - 1, (dp, me ^ j)).wait_send()
+            acc[0:8, :] = v_mp[0, 0:8, :] + v_mp[1, 0:8, :] + v_mp[2, 0:8, :] + v_mp[3, 0:8, :]
+            sum_y().start()
+        elif k == 2:
+            sum_y().wait()
+            v_z[zi] = acc[...] + v_y[...]
+            for j in (1, 2, 3):
+                sum_copy(zi, 3 + j, zpeers[j - 1], v_z).start()
+        else:
+            for j in (1, 2, 3):
+                sum_copy(zi ^ j, 3 + j, zpeers[j - 1], v_z).wait_recv()
+                sum_copy(zi, 3 + j, zpeers[j - 1], v_z).wait_send()
+            sums_ref[...] = v_z[0] + v_z[1] + v_z[2] + v_z[3]
+
+    sum_in = Scatter(place, rs_out, rs_both, rs_far, own, rs_send, rs_recv)
+    sum_out = Scatter(place, ms_out, ms_both, ms_far, m_own, ms_send, ms_recv)
+    sum_first = Scatter(place, rs_out, rs_both, rs_far, own, rt_send, rt_recv)
+
+    def finish_block(k):
+        block_ref[...] = block_ref[...] + (sum_out.finish() + vec(6))
+
+    def finish_input(k):
+        grad = sum_first.finish()
+        hat, factor = layer_hat(xp[rows(me), :].astype(f32))
+        input_ref[...] = input_ref[...] + layer_back(grad * vec(0), hat, factor)
+
+    others = (sums, finish_block, finish_input)
+
     def poll(name):
         for p, k in POLLS.get(name, ()):
+            if p >= len(blocks):
+                others[p - len(blocks)](k)
+                continue
             blocks[p].stage(k)
             if k == STAGES - 1:
                 saves[p].start()
@@ -577,12 +640,38 @@
     for t in range(3):
         stage_grad(t, dot(gate[:, t * B : (t + 1) * B], cot_all[...], TN))
         poll(f"down{t}")
+
+    def hidden_back(i, carry):
+        span = rows(me ^ (3 - i))
+        grad_u = (dot(cot_all[span, :], wdn_ref[...], NT) * du[span, :].astype(f32)).astype(bf16)
+        du[span, :] = grad_u
+        acc[8:9, :] += column_sum(grad_u.astype(f32))
+        own[...] = dot(grad_u, wup_ref[...], NT)
+        sum_in.step(i, lambda: own[...])
+        poll_at("mid", i, 4)
+        return carry
+
+    lax.fori_loop(0, 4, hidden_back, 0)
+
     for t in range(3):
         stage_grad(3 + t, dot(a2[:, t * B : (t + 1) * B], du[...], TN))
         poll(f"up{t}")
-
+    poll("up2b")
+
+    def project_down(i, carry):
+        s = me ^ (3 - i)
+        m_own[...] = dot(gate[rows(s), :], wdn_ref[...], NN)
+        sum_out.step(i, lambda: m_own[...], hold=True)
+        poll_at("mlp", i, 4)
+        return carry
+
+    lax.fori_loop(0, 4, project_down, 0)
+
+    poll("rs1")
     grad_act = sum_in.finish()
     hat, factor = layer_hat(block_ref[...])
+    acc[2:3, :] = column_sum(grad_act * hat)
+    acc[3:4, :] = column_sum(grad_act)
     cot_own = cot_all[rows(me), :].astype(f32)
     grad_h = cot_own + layer_back(grad_act * vec(3), hat, factor)
     input_ref[...] = grad_h
@@ -593,17 +682,8 @@
     acc[4:5, :] = column_sum(grad_branch.astype(f32))
     acc[5:6, :] = column_sum(cot_own)
 
-    sum_out = Scatter(place, ms_out, ms_both, ms_far, m_own, ms_send, ms_recv)
-
-    def project_down(i, carry):
-        s = me ^ (3 - i)
-        m_own[...] = dot(gate[rows(s), :], wdn_ref[...], NN)
-        sum_out.step(i, lambda: m_own[...])
-        poll_at("mlp", i, 4)
-        return carry
-
     poll("own")
-    lax.fori_loop(0, 4, project_down, 0)
+    sum_out.release()
 
     dk[...] = jnp.zeros(dk.shape, f32)
     dv[...] = jnp.zeros(dv.shape, f32)
@@ -628,13 +708,14 @@
 
         @pl.when(i == 2)
         def _():
+            poll("do")
             gather_do.forward()
 
         @pl.when(i == 3)
         def _():
             gather_do.land_far()
 
-        grad_ctx = dot(wo_ref[...], do_all[span, :], NT).astype(bf16).astype(f32)
+        grad_ctx = dot(wo_all[me], do_all[span, :], NT).astype(bf16).astype(f32)
         for h in range(3):
             here = slice(h * HD, (h + 1) * HD)
             scaled = (grad_ctx[here, :] * rinv[s, h, 0:1, :]).astype(bf16)
@@ -694,8 +775,6 @@
         poll(f"qkv{t}")
     acc[9:10, 0:192] = column_sum(dq[...].astype(f32))
     acc[9:10, 256:448] = column_sum(dvb[...].astype(f32))
-
-    sum_first = Scatter(place, rs_out, rs_both, rs_far, own, rt_send, rt_recv)
 
     def project_back(i, carry):
         s = me ^ (3 - i)
@@ -713,40 +792,9 @@
 
     lax.fori_loop(0, 4, project_back, 0)
 
-    v_mp[me] = acc[...]
-    v_copies = [remote(v_mp.at[me], v_mp.at[me], v_send.at[j - 1], v_recv.at[j - 1], (dp, me ^ j)) for j in (1, 2, 3)]
-    v_lands = [remote(v_mp.at[me ^ j], v_mp.at[me ^ j], v_send.at[j - 1], v_recv.at[j - 1], (dp, me ^ j)) for j in (1, 2, 3)]
-    for copy in v_copies:
-        copy.start()
-    poll("sums0")
-    for copy in v_lands:
-        copy.wait_recv()
-    acc[0:8, :] = v_mp[0, 0:8, :] + v_mp[1, 0:8, :] + v_mp[2, 0:8, :] + v_mp[3, 0:8, :]
-    vy_copy = remote(acc, v_y, v_send.at[3], v_recv.at[3], ypeer)
-    vy_copy.start()
-    poll("sums1")
-    vy_copy.wait_recv()
-    v_z[zi] = acc[...] + v_y[...]
-    vz_copies = [remote(v_z.at[zi], v_z.at[zi], v_send.at[3 + j], v_recv.at[3 + j], zpeers[j - 1]) for j in (1, 2, 3)]
-    vz_lands = [remote(v_z.at[zi ^ j], v_z.at[zi ^ j], v_send.at[3 + j], v_recv.at[3 + j], zpeers[j - 1]) for j in (1, 2, 3)]
-    for copy in vz_copies:
-        copy.start()
-    poll("sums2")
-
-    block_ref[...] = block_ref[...] + (sum_out.finish() + vec(6))
-    for copy in vz_lands:
-        copy.wait_recv()
-    sums_ref[...] = v_z[0] + v_z[1] + v_z[2] + v_z[3]
-
-    grad_act = sum_first.finish()
-    hat, factor = layer_hat(xp[rows(me), :].astype(f32))
-    input_ref[...] = input_ref[...] + layer_back(grad_act * vec(0), hat, factor)
-
     poll("tail")
 
-    for copy in v_copies + [vy_copy] + vz_copies:
-        copy.wait_send()
-    for gather in [gather_wo, gather_cot, gather_do] + [gather_ctx(s) for s in range(4)]:
+    for gather in [gather_wo, gather_do] + [make(s) for s in range(4) for make in (gather_ctx, gather_cot)]:
         gather.close()
     for block in blocks:
         block.close()
@@ -852,7 +900,9 @@
         shape(8, 768, dtype=f32),
         shape(16, 768, dtype=f32), shape(4, 16, 768, dtype=f32), shape(16, 768, dtype=f32), shape(4, 16, 768, dtype=f32),
     ]
-    scratch += [dma((3,))] * 4 + [dma((4, 3))] * 2 + [dma((3,))] * 8 + [dma((7,))] * 2 + [dma((10,))]
+    scratch += [dma((3,))] * 2 + [dma((4, 3))] * 4 + [dma((3,))] * 8 + [dma((7,))] * 2 + [dma((10,)), dma((14,))]
+    scratch += [shape(4 * share, 768), shape(3, 192, 768), shape(768, 768), shape(768, 768), shape(share, 768)]
+    scratch += [[shape(768)] * 7, shape(2, 192)]
     scratch += [[block_scratch(first_y, r) for first_y, r in zip(FIRST_Y, QUARTER)]]
     results = pl.pallas_call(
         layer_kernel,
@@ -865,7 +915,7 @@
             jax.ShapeDtypeStruct((1, 2, 4, 48, 384), bf16),
             jax.ShapeDtypeStruct((3, 2, 4, 48, 384), bf16),
         ],
-        in_specs=[vmem, smem] + [vmem] * 13,
+        in_specs=[anyspace, smem] + [anyspace] * 13,
         out_specs=[vmem] * 3 + [anyspace] * 4,
         scratch_shapes=scratch,
         compiler_params=pltpu.CompilerParams(

time: 143 us -> 122 us (0.85)
  Pallas kernels: 142 us -> 121 us
    pallas_call x1, Pallas kernels: 137 us -> 116 us  [per_device(): pl.pallas_call(layer_kernel, out_shape=[jax.ShapeDtypeStruct((B, 768), f3...]
where the time goes in v3:
time: 122 us
  Pallas kernels  121 us (99%)
    pallas_call x1, Pallas kernels, per_device(): pl.pallas_call(layer_kernel, out_shape=[jax.ShapeDtypeStruct((B, 768), f3...  116 us
    pallas_call x1, Pallas kernels, per_device(): pl.pallas_call(finish_kernel, out_shape=[out(share, 768), out(share, 768)...  5.51 us

profile of v3, /device:TPU:0, one launch (start us, length us, event | category | flops | bytes accessed | tf_op | source)
XLA Modules:
  0.0 122.3 jit_solution(17871203286369202571)
XLA Ops:
  0.7 116.0 %layer.1 = (f32[256,768]{1,0:T(8,128)}, f32[256,768]{1,0:T(8,128)}, f32[16,768]{1,0:T(8,128)}, bf16[3,2,4,64,384]{4,3,2,1,0:T(8,128)(2,1)}, bf16[3,2,4,64,384]{4...) custom-call(bf16[980,768]{1,0:T(8,128)(2,1)} %x_hbm.1, s32[980]{0:T(1024)} %ids_ref.1, ...), custom_call_target="tpu_custom_call" | custom-call | tf_op jit(solution)/shard_map/layer/pallas_call | solution.py:907
  116.6 5.5 %finish.1 = (f32[245,768]{1,0:T(8,128)}, f32[245,768]{1,0:T(8,128)}, f32[768]{0:T(1024)}, f32[768]{0:T(1024)}, f32[3,192,768]{2,1,0:T(8,128)}, /*index=5*/f32[2,...) custom-call(f32[256,768]{1,0:T(8,128)} %get-tuple-element.35.block_h, ...), custom_call_target="tpu_custom_call" | custom-call | tf_op jit(solution)/shard_map/finish/pallas_call | solution.py:934

commit v4 on v3

--- a/solution.py
+++ b/solution.py
@@ -55,8 +55,9 @@
         self.me, self.core, self.across = place
         self.view, self.send, self.recv = view, send, recv
 
-    def copy(self, slot, k, device):
-        return remote(self.view(slot), self.view(slot), self.send(k), self.recv(k), device)
+    def copy(self, slot, k, device, part=None):
+        view = self.view(slot) if part is None else self.view(slot).at[part]
+        return remote(view, view, self.send, self.recv(k), device)
 
     def start(self):
         self.copy(self.me, 1, self.across).start()
@@ -72,10 +73,6 @@
 
     def land_far(self):
         self.copy(self.me ^ 3, 2, self.core).wait_recv()
-
-    def close(self):
-        for k in range(3):
-            self.copy(self.me, k, self.core).wait_send()
 
 
 class Scatter:
@@ -87,7 +84,7 @@
     def copy(self, k):
         src = self.out.at[k]
         dst = self.far if k == 1 else self.both.at[k // 2]
-        return remote(src, dst, self.send.at[k], self.recv.at[k], self.across if k == 1 else self.core)
+        return remote(src, dst, self.send, self.recv.at[k], self.across if k == 1 else self.core)
 
     def step(self, i, value, hold=False):
         @pl.when(i == 0)
@@ -122,8 +119,7 @@
         self.copy(2).wait_recv()
         self.copy(1).wait_recv()
         total = self.own[...] + self.both[1].astype(f32) + self.far[...].astype(f32)
-        for k in range(3):
-            self.copy(k).wait_send()
+        remote(self.out, self.out, self.send, self.recv.at[0], self.core).wait_send()
         return total
 
 
@@ -132,24 +128,22 @@
         self.zi, self.yi, self.over, self.above, self.below = spot
         self.first_y = first_y
         self.part, self.ybuf, self.up, self.down, self.whole, self.send, self.recv = refs
-        self.sent = []
-
-    def copy(self, src, dst, k, device):
-        return remote(src, dst, self.send.at[k], self.recv.at[k], device)
+
+    def copy(self, src, dst, k, slot, device):
+        return remote(src, dst, self.send.at[k], self.recv.at[slot], device)
 
     def begin(self, condition, make):
-        self.sent.append((condition, make))
         if condition is None:
             make().start()
         else:
             pl.when(condition())(lambda: make().start())
 
     def close(self):
-        for condition, make in self.sent:
-            if condition is None:
-                make().wait_send()
-            else:
-                pl.when(condition())(lambda make=make: make().wait_send())
+        all_along = self.whole.at[self.yi] if self.first_y else self.whole
+        all_over = self.whole if self.first_y else self.whole.at[:, 0]
+        pl.when(self.zi < 3)(lambda: self.copy(all_along, all_along, 1, 1, self.above).wait_send())
+        pl.when(self.zi > 0)(lambda: self.copy(all_along, all_along, 2, 2, self.below).wait_send())
+        self.copy(all_over, all_over, 0, 0, self.over).wait_send()
 
     def chunks(self, first, count):
         return self.part.at[self.yi if self.first_y else slice(None), pl.ds(first, count)]
@@ -166,10 +160,10 @@
         return self.whole.at[self.yi if self.first_y else slice(None), chunk]
 
     def copy_up(self, first, count, src):
-        return self.copy(src, self.rising(first, count), 1, self.above)
+        return self.copy(src, self.rising(first, count), 1, 1, self.above)
 
     def copy_down(self, first, count, src):
-        return self.copy(src, self.falling(first, count), 2, self.below)
+        return self.copy(src, self.falling(first, count), 2, 2, self.below)
 
     def at(self, z):
         return lambda: self.zi == z
@@ -224,38 +218,35 @@
                 store(z, value)
 
     def back(self, d):
-        for sign, base, ahead, room in ((-1, 3, self.above, lambda: self.zi < 3), (1, 6, self.below, lambda: self.zi > 0)):
+        for sign, k, ahead, room in ((-1, 1, self.above, lambda: self.zi < 3), (1, 2, self.below, lambda: self.zi > 0)):
 
             def here(sign=sign):
                 return self.zi >= d if sign < 0 else self.zi <= 3 - d
 
-            def view(sign=sign):
-                return self.result(self.zi + sign * d)
+            def move(sign=sign, k=k, ahead=ahead):
+                chunk = self.zi + sign * d
+                view = self.result(chunk)
+                return self.copy(view, view, k, 3 + chunk, ahead)
 
             if d > 0:
 
                 @pl.when(here())
                 def _():
-                    self.copy(view(), view(), base + d - 1, ahead).wait_recv()
+                    move().wait_recv()
 
             if d < 3:
-                self.begin(
-                    lambda room=room, here=here: room() & here(),
-                    lambda view=view, base=base, ahead=ahead: self.copy(view(), view(), base + d, ahead),
-                )
+                self.begin(lambda room=room, here=here: room() & here(), move)
             if self.first_y and (d > 0 or sign < 0):
-                self.begin(
-                    here, lambda view=view, sign=sign: self.copy_over(self.yi, self.zi + sign * d)
-                )
+                self.begin(here, lambda sign=sign: self.copy_over(self.yi, self.zi + sign * d))
 
     def copy_over(self, half, chunk):
         view = self.whole.at[half, chunk]
-        return self.copy(view, view, 9 + (chunk if self.first_y else 0), self.over)
+        return self.copy(view, view, 0, 7, self.over)
 
     def sum_over(self):
         if self.first_y:
-            return self.copy(self.part.at[1 - self.yi], self.ybuf, 0, self.over)
-        return self.copy(self.part.at[1 - self.yi, self.zi], self.ybuf, 0, self.over)
+            return self.copy(self.part.at[1 - self.yi], self.ybuf, 0, 0, self.over)
+        return self.copy(self.part.at[1 - self.yi, self.zi], self.ybuf, 0, 0, self.over)
 
     def stage(self, k):
         if self.first_y:
@@ -283,8 +274,8 @@
             elif k in (5, 6, 7):
                 self.back(k - 4)
             else:
-                for c in range(4):
-                    self.copy_over(1 - self.yi, c).wait_recv()
+                other = self.whole.at[1 - self.yi]
+                self.copy(other, other, 0, 7, self.over).wait_recv()
         else:
             if k in (0, 1, 2):
                 self.hop(k + 1)
@@ -321,35 +312,38 @@
     "rs1": ((2, 1), (1, 2),),
     "own": ((0, 2), (3, 1),),
     "attend0": ((1, 3), (2, 2),),
-    "attend3": ((1, 4), (0, 3), (3, 2),),
-    "attend4": ((2, 3), (4, 1),),
-    "do": ((5, 1), (1, 5),),
-    "attend6": ((0, 4), (2, 4), (3, 3),),
-    "attend7": ((1, 6), (4, 2),),
-    "attend9": ((0, 5), (3, 4), (5, 2),),
-    "attend10": ((1, 7), (2, 5), (4, 3),),
+    "attend3": ((0, 3), (1, 4),),
+    "attend4": ((2, 3), (3, 2),),
+    "attend5": ((4, 1),),
+    "do": ((5, 1), (1, 5), (0, 4),),
+    "attend6": ((2, 4), (3, 3),),
+    "attend8": ((1, 6), (4, 2),),
+    "attend9": ((0, 5), (3, 4),),
+    "attend10": ((1, 7), (5, 2),),
+    "attend11": ((2, 5), (4, 3),),
     "out": ((6, 0),),
     "qkv0": ((7, 0),),
-    "qkv1": ((1, 8), (0, 6), (8, 0),),
-    "qkv2": ((9, 0),),
+    "qkv1": ((0, 6), (1, 8),),
+    "qkv2": ((8, 0), (9, 0),),
     "first0": ((3, 5),),
     "first2": ((4, 4), (5, 3),),
-    "first3": ((2, 6), (6, 1),),
-    "tail": ((10, 0), (11, 0), (0, 7), (3, 6), (7, 1), (4, 5), (5, 4), (6, 2), (2, 7), (8, 1), (0, 8), (7, 2), (3, 7), (12, 0), (4, 6), (6, 3), (9, 1), (10, 1), (5, 5), (8, 2), (7, 3), (4, 7), (6, 4), (9, 2), (5, 6), (8, 3), (7, 4), (6, 5), (2, 8), (5, 7), (9, 3), (3, 8), (8, 4), (7, 5), (6, 6), (10, 2), (9, 4), (8, 5), (4, 8), (7, 6), (6, 7), (5, 8), (10, 3), (9, 5), (7, 7), (8, 6), (6, 8), (9, 6), (8, 7), (7, 8), (9, 7), (8, 8), (9, 8),),
+    "first3": ((2, 6),),
+    "tail": ((10, 0), (11, 0), (6, 1), (0, 7), (3, 6), (4, 5), (5, 4), (7, 1), (2, 7), (6, 2), (0, 8), (8, 1), (3, 7), (12, 0), (4, 6), (6, 3), (7, 2), (10, 1), (5, 5), (9, 1), (8, 2), (4, 7), (6, 4), (7, 3), (9, 2), (5, 6), (7, 4), (8, 3), (2, 8), (6, 5), (5, 7), (3, 8), (9, 3), (8, 4), (7, 5), (6, 6), (10, 2), (9, 4), (4, 8), (8, 5), (7, 6), (6, 7), (5, 8), (10, 3), (9, 5), (7, 7), (8, 6), (6, 8), (9, 6), (8, 7), (7, 8), (9, 7), (8, 8), (9, 8),),
 }
 
 
 def layer_kernel(
-    x_hbm, ids_ref, gain_a, shift_a, bias_qv, bias_out, gain_b, shift_b, bias_up, bias_down,
+    x_hbm, ids_hbm, gain_a, shift_a, bias_qv, bias_out, gain_b, shift_b, bias_up, bias_down,
     wqkv_hbm, wo_hbm, wup_hbm, wdn_hbm, cot_hbm,
-    block_ref, input_ref, sums_ref, down_hbm, up_hbm, out_hbm, qkv_hbm,
+    block_hbm, input_hbm, sums_hbm, down_hbm, up_hbm, out_hbm, qkv_hbm,
     xp, stage, a1, keys, values, keys_t, values_t, qz_t, qz, kid, qid, probs, probs_last, rinv, ctx_t, ctx_all,
     wo_all, cot_all, a2, gate, du, do_all, dcz_t, dcz, delta, dq, dk, dv, dkb, dvb, own,
     rs_out, rs_both, rs_far, ms_out, ms_both, ms_far, m_own,
     vec_ref, acc, v_mp, v_y, v_z,
     wo_send, wo_recv, cot_send, cot_recv, ctx_send, ctx_recv, do_send, do_recv,
     rs_send, rs_recv, ms_send, ms_recv, rt_send, rt_recv,
-    v_send, v_recv, local_sem, load_sem, x_ref, wqkv_ref, wup_ref, wdn_ref, cot_ref, vec_raw, qv_raw, block_refs,
+    v_send, v_recv, local_sem, load_sem, x_ref, wqkv_ref, wup_ref, wdn_ref, cot_ref, vec_raw, qv_raw,
+    block_ref, input_ref, sums_ref, ids_ref, block_refs,
 ):
     dp, me = lax.axis_index("dp"), lax.axis_index("mp")
     core, across, diagonal = (dp, me ^ 1), (dp, me ^ 2), (dp, me ^ 3)
@@ -370,31 +364,26 @@
     def vec(r, width=None):
         return vec_ref[r : r + 1, :] if width is None else vec_ref[r : r + 1, width[0] : width[1]]
 
-    pairs = [(cot_hbm, cot_ref), (x_hbm, x_ref), (wo_hbm, wo_all.at[me]), (bias_qv, qv_raw)]
+    pairs = [(wo_hbm, wo_all.at[me]), (cot_hbm, cot_ref), (x_hbm, x_ref), (bias_qv, qv_raw)]
     pairs += list(zip((gain_a, shift_a, bias_out, gain_b, shift_b, bias_up, bias_down), vec_raw))
-    pairs += [(wqkv_hbm, wqkv_ref), (wup_hbm, wup_ref), (wdn_hbm, wdn_ref)]
+    pairs += [(wqkv_hbm, wqkv_ref), (wup_hbm, wup_ref), (wdn_hbm, wdn_ref), (ids_hbm, ids_ref)]
     loads = [pltpu.make_async_copy(src, dst, load_sem.at[k]) for k, (src, dst) in enumerate(pairs)]
     for load in loads:
         load.start()
     pl.semaphore_wait(barrier, len(partners))
 
-    gather_wo = Gather(place, lambda s: wo_all.at[s], lambda k: wo_send.at[k], lambda k: wo_recv.at[k])
-    loads[2].wait()
+    gather_wo = Gather(place, lambda s: wo_all.at[s], wo_send.at[0], lambda k: wo_recv.at[k])
+    loads[0].wait()
     gather_wo.start()
 
-    def gather_cot(q):
-        return Gather(
-            place,
-            lambda s: cot_all.at[pl.ds(pl.multiple_of(s * B + q * 64, 64), 64)],
-            lambda k: cot_send.at[q, k],
-            lambda k: cot_recv.at[q, k],
-        )
-
-    loads[0].wait()
+    gather_cot = Gather(place, lambda s: cot_all.at[rows(s)], cot_send.at[0], lambda k: cot_recv.at[k])
+
+    loads[1].wait()
     stage[240:256, :] = jnp.zeros((16, 768), f32)
     stage[0:share, :] = cot_ref[...].astype(f32)
     cot_all[rows(me), :] = stage[0:B, :].astype(bf16)
-    gather_cot(0).start()
+    gather_cot.copy(me, 1, across, pl.ds(0, 64)).start()
+    gather_cot.copy(me, 0, core).start()
     acc[...] = jnp.zeros(acc.shape, f32)
     for k in range(3, 11):
         loads[k].wait()
@@ -402,7 +391,7 @@
         vec_ref[r : r + 1, :] = ref[...].astype(f32).reshape(1, 768)
     vec_ref[7:8, 0:192] = qv_raw[0:1, :].astype(f32)
     vec_ref[7:8, 256:448] = qv_raw[1:2, :].astype(f32)
-    loads[1].wait()
+    loads[2].wait()
 
     row_in = lax.broadcasted_iota(i32, (B, 768), 0)
     for s in range(4):
@@ -412,6 +401,7 @@
         moved = stage[s * share - first : s * share - first + B, :]
         xp[s * B : (s + 1) * B, :] = jnp.where(row_in < share, moved, 0.0).astype(bf16)
 
+    loads[14].wait()
     two_images = (ids_ref[0] == ids_ref[BIG - 1]).astype(i32)
 
     def image_of(index, shard, pad):
@@ -457,7 +447,7 @@
 
     def gather_ctx(s):
         return Gather(
-            place, lambda j: ctx_all.at[j, s], lambda k: ctx_send.at[s, k], lambda k: ctx_recv.at[s, k]
+            place, lambda j: ctx_all.at[j, s], ctx_send.at[0], lambda k: ctx_recv.at[s, k]
         )
 
     def attend(s, h, low, high, qlow, qhigh, store):
@@ -520,7 +510,7 @@
     send_ctx(3)
 
     for q in (1, 2, 3):
-        gather_cot(q).start()
+        gather_cot.copy(me, 1, across, pl.ds(q * 64, 64)).start()
     gather_wo.land_core()
     gather_wo.land_far()
     for s in range(4):
@@ -562,23 +552,25 @@
 
     lax.fori_loop(0, 4, middle, 0)
 
-    for q in range(4):
-        gather_cot(q).forward()
-    for q in range(4):
-        gather_cot(q).land_core()
-        gather_cot(q).land_far()
+    gather_cot.forward()
+    gather_cot.land_core()
+    gather_cot.land_far()
 
     blocks = [Reduce(spot, first_y, refs) for first_y, refs in zip(FIRST_Y, block_refs)]
     homes = [down_hbm.at[p] for p in range(3)] + [up_hbm.at[p] for p in range(3)]
     homes += [out_hbm.at[0]] + [qkv_hbm.at[p] for p in range(3)]
-    saves = [pltpu.make_async_copy(blocks[p].whole, homes[p], local_sem.at[p]) for p in range(10)]
+    tensor = (0, 0, 0, 1, 1, 1, 2, 3, 3, 3)
+    saves = [pltpu.make_async_copy(blocks[p].whole, homes[p], local_sem.at[tensor[p]]) for p in range(10)]
+    save_block = pltpu.make_async_copy(block_ref, block_hbm, local_sem.at[4])
+    save_input = pltpu.make_async_copy(input_ref, input_hbm, local_sem.at[5])
+    save_sums = pltpu.make_async_copy(sums_ref, sums_hbm, local_sem.at[6])
 
     def sum_copy(slot, k, device, ref=v_mp):
         view = ref.at[slot]
-        return remote(view, view, v_send.at[k], v_recv.at[k], device)
+        return remote(view, view, v_send.at[0 if k < 3 else 2], v_recv.at[k], device)
 
     def sum_y():
-        return remote(acc, v_y, v_send.at[3], v_recv.at[3], ypeer)
+        return remote(acc, v_y, v_send.at[1], v_recv.at[3], ypeer)
 
     def sums(k):
         if k == 0:
@@ -588,7 +580,6 @@
         elif k == 1:
             for j in (1, 2, 3):
                 sum_copy(me ^ j, j - 1, (dp, me ^ j)).wait_recv()
-                sum_copy(me, j - 1, (dp, me ^ j)).wait_send()
             acc[0:8, :] = v_mp[0, 0:8, :] + v_mp[1, 0:8, :] + v_mp[2, 0:8, :] + v_mp[3, 0:8, :]
             sum_y().start()
         elif k == 2:
@@ -599,20 +590,24 @@
         else:
             for j in (1, 2, 3):
                 sum_copy(zi ^ j, 3 + j, zpeers[j - 1], v_z).wait_recv()
-                sum_copy(zi, 3 + j, zpeers[j - 1], v_z).wait_send()
             sums_ref[...] = v_z[0] + v_z[1] + v_z[2] + v_z[3]
-
-    sum_in = Scatter(place, rs_out, rs_both, rs_far, own, rs_send, rs_recv)
-    sum_out = Scatter(place, ms_out, ms_both, ms_far, m_own, ms_send, ms_recv)
-    sum_first = Scatter(place, rs_out, rs_both, rs_far, own, rt_send, rt_recv)
+            save_sums.start()
+            sum_copy(slice(0, 3), 0, core).wait_send()
+            sum_copy(slice(0, 3), 4, core, v_z).wait_send()
+
+    sum_in = Scatter(place, rs_out, rs_both, rs_far, own, rs_send.at[0], rs_recv)
+    sum_out = Scatter(place, ms_out, ms_both, ms_far, m_own, ms_send.at[0], ms_recv)
+    sum_first = Scatter(place, rs_out, rs_both, rs_far, own, rt_send.at[0], rt_recv)
 
     def finish_block(k):
         block_ref[...] = block_ref[...] + (sum_out.finish() + vec(6))
+        save_block.start()
 
     def finish_input(k):
         grad = sum_first.finish()
         hat, factor = layer_hat(xp[rows(me), :].astype(f32))
         input_ref[...] = input_ref[...] + layer_back(grad * vec(0), hat, factor)
+        save_input.start()
 
     others = (sums, finish_block, finish_input)
 
@@ -677,7 +672,7 @@
     input_ref[...] = grad_h
     grad_branch = grad_h.astype(bf16)
     do_all[rows(me), :] = grad_branch
-    gather_do = Gather(place, lambda s: do_all.at[rows(s)], lambda k: do_send.at[k], lambda k: do_recv.at[k])
+    gather_do = Gather(place, lambda s: do_all.at[rows(s)], do_send.at[0], lambda k: do_recv.at[k])
     gather_do.start()
     acc[4:5, :] = column_sum(grad_branch.astype(f32))
     acc[5:6, :] = column_sum(cot_own)
@@ -794,11 +789,18 @@
 
     poll("tail")
 
-    for gather in [gather_wo, gather_do] + [make(s) for s in range(4) for make in (gather_ctx, gather_cot)]:
-        gather.close()
+    for gather, total in (
+        (gather_wo, wo_all.at[0:3]),
+        (gather_cot, cot_all.at[0:768]),
+        (gather_do, do_all.at[0:768]),
+        (gather_ctx(0), ctx_all.at[0:3]),
+    ):
+        remote(total, total, gather.send, gather.recv(0), core).wait_send()
     for block in blocks:
         block.close()
-    for save in saves:
+    for k, whole in enumerate((down_hbm, up_hbm, out_hbm, qkv_hbm)):
+        pltpu.make_async_copy(whole, whole, local_sem.at[k]).wait()
+    for save in (save_block, save_input, save_sums):
         save.wait()
 
 
@@ -872,7 +874,7 @@
     shift_second, up_weight, up_bias, down_weight, down_bias, cotangent,
 ):
     share = cotangent.shape[0]
-    vmem, smem, anyspace = (pl.BlockSpec(memory_space=m) for m in (pltpu.VMEM, pltpu.SMEM, pl.ANY))
+    vmem, anyspace = (pl.BlockSpec(memory_space=m) for m in (pltpu.VMEM, pl.ANY))
 
     def shape(*dims, dtype=bf16):
         return pltpu.VMEM(dims, dtype)
@@ -882,7 +884,7 @@
     def block_scratch(first_y, r):
         over = shape(4, r, 384) if first_y else shape(r, 384)
         along = shape(3, r, 384) if first_y else shape(2, 3, r, 384)
-        return [shape(2, 4, r, 384), over, along, along, shape(2, 4, r, 384), dma((13,)), dma((13,))]
+        return [shape(2, 4, r, 384), over, along, along, shape(2, 4, r, 384), dma((3,)), dma((8,))]
 
     scratch = [
         shape(1024, 768), shape(272, 768, dtype=f32), shape(1024, 768),
@@ -900,9 +902,12 @@
         shape(8, 768, dtype=f32),
         shape(16, 768, dtype=f32), shape(4, 16, 768, dtype=f32), shape(16, 768, dtype=f32), shape(4, 16, 768, dtype=f32),
     ]
-    scratch += [dma((3,))] * 2 + [dma((4, 3))] * 4 + [dma((3,))] * 8 + [dma((7,))] * 2 + [dma((10,)), dma((14,))]
+    one, three = dma((1,)), dma((3,))
+    scratch += [one, three, one, three, one, dma((4, 3)), one, three] + [one, three] * 3
+    scratch += [three, dma((7,)), dma((7,)), dma((15,))]
     scratch += [shape(4 * share, 768), shape(3, 192, 768), shape(768, 768), shape(768, 768), shape(share, 768)]
-    scratch += [[shape(768)] * 7, shape(2, 192)]
+    scratch += [[shape(768)] * 7, shape(2, 192), shape(B, 768, dtype=f32), shape(B, 768, dtype=f32)]
+    scratch += [shape(16, 768, dtype=f32), pltpu.SMEM(image_of_row.shape, i32)]
     scratch += [[block_scratch(first_y, r) for first_y, r in zip(FIRST_Y, QUARTER)]]
     results = pl.pallas_call(
         layer_kernel,
@@ -915,8 +920,8 @@
             jax.ShapeDtypeStruct((1, 2, 4, 48, 384), bf16),
             jax.ShapeDtypeStruct((3, 2, 4, 48, 384), bf16),
         ],
-        in_specs=[anyspace, smem] + [anyspace] * 13,
-        out_specs=[vmem] * 3 + [anyspace] * 4,
+        in_specs=[anyspace] * 15,
+        out_specs=[anyspace] * 7,
         scratch_shapes=scratch,
         compiler_params=pltpu.CompilerParams(
             collective_id=0, has_side_effects=True, vmem_limit_bytes=60 * 2**20

time: 122 us -> 119 us (0.975)
  Pallas kernels: 121 us -> 119 us
    pallas_call x1, Pallas kernels: 116 us -> 113 us  [per_device(): pl.pallas_call(layer_kernel, out_shape=[jax.ShapeDtypeStruct((B, 768), f3...]
where the time goes in v4:
time: 119 us
  Pallas kernels  119 us (100%)
    pallas_call x1, Pallas kernels, per_device(): pl.pallas_call(layer_kernel, out_shape=[jax.ShapeDtypeStruct((B, 768), f3...  113 us
    pallas_call x1, Pallas kernels, per_device(): pl.pallas_call(finish_kernel, out_shape=[out(share, 768), out(share, 768)...  5.51 us

profile of v4, /device:TPU:0, one launch (start us, length us, event | category | flops | bytes accessed | tf_op | source)
XLA Modules:
  0.0 119.3 jit_solution(2539416291488594955)
XLA Ops:
  0.7 113.0 %layer.1 = (f32[256,768]{1,0:T(8,128)}, f32[256,768]{1,0:T(8,128)}, f32[16,768]{1,0:T(8,128)}, bf16[3,2,4,64,384]{4,3,2,1,0:T(8,128)(2,1)}, bf16[3,2,4,64,384]{4...) custom-call(bf16[980,768]{1,0:T(8,128)(2,1)} %x_hbm.1, s32[980]{0:T(1024)} %ids_hbm.1, ...), custom_call_target="tpu_custom_call" | custom-call | tf_op jit(solution)/shard_map/layer/pallas_call | solution.py:912
  113.7 5.5 %finish.1 = (f32[245,768]{1,0:T(8,128)}, f32[245,768]{1,0:T(8,128)}, f32[768]{0:T(1024)}, f32[768]{0:T(1024)}, f32[3,192,768]{2,1,0:T(8,128)}, /*index=5*/f32[2,...) custom-call(f32[256,768]{1,0:T(8,128)} %get-tuple-element.35.block_h, ...), custom_call_target="tpu_custom_call" | custom-call | tf_op jit(solution)/shard_map/finish/pallas_call | solution.py:939

commit v5 on v4

--- a/solution.py
+++ b/solution.py
@@ -298,7 +298,7 @@
                 self.back(k - 5)
 
 
-FIRST_Y = (False, True, True, True, True, True, True, True, True, True)
+FIRST_Y = (True, False, True, True, True, True, True, True, True, False)
 QUARTER = (64,) * 6 + (48,) * 4
 STAGES = 9
 
@@ -306,29 +306,31 @@
     "down0": ((0, 0),),
     "down1": ((1, 0),),
     "down2": ((2, 0),),
-    "up0": ((3, 0), (1, 1),),
+    "mid3": ((0, 1),),
+    "up0": ((3, 0),),
     "up1": ((4, 0),),
-    "up2": ((0, 1), (5, 0),),
-    "rs1": ((2, 1), (1, 2),),
-    "own": ((0, 2), (3, 1),),
-    "attend0": ((1, 3), (2, 2),),
-    "attend3": ((0, 3), (1, 4),),
-    "attend4": ((2, 3), (3, 2),),
-    "attend5": ((4, 1),),
-    "do": ((5, 1), (1, 5), (0, 4),),
-    "attend6": ((2, 4), (3, 3),),
-    "attend8": ((1, 6), (4, 2),),
-    "attend9": ((0, 5), (3, 4),),
-    "attend10": ((1, 7), (5, 2),),
-    "attend11": ((2, 5), (4, 3),),
-    "out": ((6, 0),),
+    "up2": ((5, 0), (1, 1),),
+    "mlp2": ((2, 1),),
+    "rs1": ((0, 2),),
+    "own": ((3, 1), (2, 2), (1, 2),),
+    "attend0": ((0, 3),),
+    "after0": ((4, 1),),
+    "prep1": ((3, 2), (2, 3), (1, 3),),
+    "attend1": ((0, 4),),
+    "after1": ((5, 1),),
+    "do": ((2, 4), (4, 2), (1, 4), (3, 3),),
+    "prep2": ((0, 5),),
+    "attend2": ((3, 4), (1, 5), (5, 2),),
+    "after2": ((4, 3), (2, 5),),
+    "prep3": ((0, 6),),
+    "attend3": ((3, 5),),
+    "out": ((6, 0), (1, 6),),
     "qkv0": ((7, 0),),
-    "qkv1": ((0, 6), (1, 8),),
-    "qkv2": ((8, 0), (9, 0),),
-    "first0": ((3, 5),),
-    "first2": ((4, 4), (5, 3),),
-    "first3": ((2, 6),),
-    "tail": ((10, 0), (11, 0), (6, 1), (0, 7), (3, 6), (4, 5), (5, 4), (7, 1), (2, 7), (6, 2), (0, 8), (8, 1), (3, 7), (12, 0), (4, 6), (6, 3), (7, 2), (10, 1), (5, 5), (9, 1), (8, 2), (4, 7), (6, 4), (7, 3), (9, 2), (5, 6), (7, 4), (8, 3), (2, 8), (6, 5), (5, 7), (3, 8), (9, 3), (8, 4), (7, 5), (6, 6), (10, 2), (9, 4), (4, 8), (8, 5), (7, 6), (6, 7), (5, 8), (10, 3), (9, 5), (7, 7), (8, 6), (6, 8), (9, 6), (8, 7), (7, 8), (9, 7), (8, 8), (9, 8),),
+    "qkv1": ((8, 0), (4, 4),),
+    "qkv2": ((9, 0),),
+    "first0": ((5, 3),),
+    "first1": ((2, 6), (0, 7), (3, 6),),
+    "tail": ((11, 0), (10, 0), (1, 7), (6, 1), (4, 5), (5, 4), (9, 1), (2, 7), (7, 1), (3, 7), (6, 2), (1, 8), (8, 1), (4, 6), (12, 0), (9, 2), (7, 2), (5, 5), (0, 8), (10, 1), (6, 3), (4, 7), (8, 2), (9, 3), (2, 8), (7, 3), (3, 8), (5, 6), (6, 4), (7, 4), (8, 3), (5, 7), (6, 5), (4, 8), (10, 2), (7, 5), (9, 4), (8, 4), (6, 6), (5, 8), (9, 5), (10, 3), (7, 6), (6, 7), (8, 5), (9, 6), (7, 7), (6, 8), (8, 6), (9, 7), (7, 8), (8, 7), (9, 8), (8, 8),),
 }
 
 
@@ -337,7 +339,7 @@
     wqkv_hbm, wo_hbm, wup_hbm, wdn_hbm, cot_hbm,
     block_hbm, input_hbm, sums_hbm, down_hbm, up_hbm, out_hbm, qkv_hbm,
     xp, stage, a1, keys, values, keys_t, values_t, qz_t, qz, kid, qid, probs, probs_last, rinv, ctx_t, ctx_all,
-    wo_all, cot_all, a2, gate, du, do_all, dcz_t, dcz, delta, dq, dk, dv, dkb, dvb, own,
+    wo_all, cot_all, a2, gate, du, do_all, dcz_t, dcz, delta, dk, dv, own,
     rs_out, rs_both, rs_far, ms_out, ms_both, ms_far, m_own,
     vec_ref, acc, v_mp, v_y, v_z,
     wo_send, wo_recv, cot_send, cot_recv, ctx_send, ctx_recv, do_send, do_recv,
@@ -382,7 +384,6 @@
     stage[240:256, :] = jnp.zeros((16, 768), f32)
     stage[0:share, :] = cot_ref[...].astype(f32)
     cot_all[rows(me), :] = stage[0:B, :].astype(bf16)
-    gather_cot.copy(me, 1, across, pl.ds(0, 64)).start()
     gather_cot.copy(me, 0, core).start()
     acc[...] = jnp.zeros(acc.shape, f32)
     for k in range(3, 11):
@@ -450,19 +451,22 @@
             place, lambda j: ctx_all.at[j, s], ctx_send.at[0], lambda k: ctx_recv.at[s, k]
         )
 
-    def attend(s, h, low, high, qlow, qhigh, store):
-        lanes = pl.ds(pl.multiple_of(h * B + qlow, 128), qhigh - qlow)
-        scores = dot(keys[low:high, :], qz_t[s, :, lanes], NN)
+    def attend(s, low, high, qlow, qhigh):
+        width = qhigh - qlow
+        wanted = qz_t[s]
+        if width < B:
+            wanted = jnp.concatenate([wanted[:, h * B + qlow : h * B + qhigh] for h in range(3)], axis=1)
+        scores = dot(keys[low:high, :], wanted, NN)
         same = kid[low:high, qlow:qhigh] == qid[s, 0:1, qlow:qhigh]
-        scores = jnp.where(same, scores, -1e30)
-        top = jnp.max(scores, axis=0, keepdims=True)
-        weights = jnp.exp(scores - top)
+        scores = jnp.where(jnp.concatenate([same] * 3, axis=1), scores, -1e30)
+        weights = jnp.exp(scores - jnp.max(scores, axis=0, keepdims=True))
         inverse = 1.0 / jnp.sum(weights, axis=0, keepdims=True)
         weights = weights.astype(bf16)
-        store(lanes, weights)
-        rinv[s, h, 0:1, qlow:qhigh] = inverse
-        head = pl.ds(pl.multiple_of(h * HD, HD), HD)
-        return (dot(values_t[head, low:high], weights, NN) * inverse).astype(bf16)
+        mixed = dot(values_t[:, low:high], weights, NN) * inverse
+        for h in range(3):
+            rinv[s, h, 0:1, qlow:qhigh] = inverse[:, h * width : (h + 1) * width]
+        heads = [mixed[h * HD : (h + 1) * HD, h * width : (h + 1) * width] for h in range(3)]
+        return weights, jnp.concatenate(heads, axis=0).astype(bf16)
 
     def send_ctx(s):
         span = rows(s)
@@ -473,15 +477,7 @@
         gather_ctx(s).start()
 
     def attend_top(s, carry):
-        def head(h, inner):
-            def store(lanes, weights):
-                probs[s, :, lanes] = weights
-
-            here = pl.ds(pl.multiple_of(h * HD, HD), HD)
-            ctx_t[here, rows(s)] = attend(s, h, 0, TOP, 0, B, store)
-            return inner
-
-        lax.fori_loop(0, 3, head, 0)
+        probs[s], ctx_t[:, rows(s)] = attend(s, 0, TOP, 0, B)
         send_ctx(s)
 
         @pl.when(s == 1)
@@ -492,24 +488,15 @@
 
     lax.fori_loop(0, 3, attend_top, 0)
 
-    def attend_last(h, carry):
-        here = pl.ds(pl.multiple_of(h * HD, HD), HD)
-
-        def store_left(lanes, weights):
-            probs_last[:, lanes] = weights
-
-        def store_right(lanes, weights):
-            probs_last[0:768, lanes] = jnp.zeros((768, 128), bf16)
-            probs_last[768:1024, lanes] = weights
-
-        ctx_t[here, 768:896] = attend(3, h, 0, 1024, 0, 128, store_left)
-        ctx_t[here, 896:1024] = attend(3, h, 768, 1024, 128, 256, store_right)
-        return carry
-
-    lax.fori_loop(0, 3, attend_last, 0)
+    left, ctx_t[:, 768:896] = attend(3, 0, 1024, 0, 128)
+    right, ctx_t[:, 896:1024] = attend(3, 768, 1024, 128, 256)
+    for h in range(3):
+        probs_last[:, h * B : h * B + 128] = left[:, h * 128 : (h + 1) * 128]
+        probs_last[0:768, h * B + 128 : (h + 1) * B] = jnp.zeros((768, 128), bf16)
+        probs_last[768:1024, h * B + 128 : (h + 1) * B] = right[:, h * 128 : (h + 1) * 128]
     send_ctx(3)
 
-    for q in (1, 2, 3):
+    for q in range(4):
         gather_cot.copy(me, 1, across, pl.ds(q * 64, 64)).start()
     gather_wo.land_core()
     gather_wo.land_far()
@@ -680,18 +667,17 @@
     poll("own")
     sum_out.release()
 
+    dq, dkb, dvb = (slice(256 * k, 256 * k + 192) for k in range(3))
     dk[...] = jnp.zeros(dk.shape, f32)
     dv[...] = jnp.zeros(dv.shape, f32)
 
-    def back_head(s, h, low, high, qlow, qhigh, ref):
-        lanes = pl.ds(pl.multiple_of(h * B + qlow, 128), qhigh - qlow)
-        head = pl.ds(pl.multiple_of(h * HD, HD), HD)
-        weights = ref[low:high, lanes]
-        grad_probs = dot(values[low:high, :], dcz_t[:, lanes], NN)
-        grad_scores = weights.astype(f32) * (grad_probs - delta[h, 0:1, qlow:qhigh])
+    def back_heads(weights, low, high, wanted, center):
+        width = weights.shape[1] // 3
+        grad_scores = weights.astype(f32) * (dot(values[low:high, :], wanted, NN) - center)
         grad_scores = grad_scores.astype(bf16)
-        ref[low:high, lanes] = grad_scores
-        return dot(keys_t[head, low:high], grad_scores, NN)
+        mixed = dot(keys_t[:, low:high], grad_scores, NN)
+        heads = [mixed[h * HD : (h + 1) * HD, h * width : (h + 1) * width] for h in range(3)]
+        return grad_scores, jnp.concatenate(heads, axis=0)
 
     def back_block(i, carry):
         s = me ^ i
@@ -714,7 +700,7 @@
         for h in range(3):
             here = slice(h * HD, (h + 1) * HD)
             scaled = (grad_ctx[here, :] * rinv[s, h, 0:1, :]).astype(bf16)
-            delta[h, 0:1, :] = column_sum(scaled.astype(f32) * ctx_t[here, span].astype(f32))
+            delta[0:1, h * B : (h + 1) * B] = column_sum(scaled.astype(f32) * ctx_t[here, span].astype(f32))
             dcz_t[here, h * B : (h + 1) * B] = scaled
             turned = jnp.concatenate([scaled, jnp.zeros((HD, B), bf16)], axis=0).T.astype(f32)
             wide = jnp.concatenate([turned, turned], axis=1)[:, 0:192]
@@ -730,32 +716,38 @@
         def _():
             dv[...] += dot(probs_last[...], dcz[...], NN)
 
-        def head(h, inner):
-            here = pl.ds(pl.multiple_of(h * HD, HD), HD)
-
-            @pl.when(s != 3)
-            def _():
-                stage[here, 0:B] = back_head(s, h, 0, TOP, 0, B, probs.at[s])
-
-            @pl.when(s == 3)
-            def _():
-                stage[here, 0:128] = back_head(s, h, 0, 1024, 0, 128, probs_last)
-                stage[here, 128:256] = back_head(s, h, 768, 1024, 128, 256, probs_last)
-
-            poll_at("attend", i * 3 + h, 12)
-            return inner
-
-        lax.fori_loop(0, 3, head, 0)
+        poll_at("prep", i, 4)
 
         @pl.when(s != 3)
         def _():
+            probs[s], stage[0:192, 0:B] = back_heads(probs[s], 0, TOP, dcz_t[...], delta[0:1, :])
+
+        @pl.when(s == 3)
+        def _():
+            def side(ref, low, high, qlow):
+                parts = [ref[low:high, h * B + qlow : h * B + qlow + 128] for h in range(3)]
+                return jnp.concatenate(parts, axis=1)
+
+            for low, qlow in ((0, 0), (768, 128)):
+                wanted, center = side(dcz_t, 0, 192, qlow), side(delta, 0, 1, qlow)
+                grad_scores, grad_q = back_heads(side(probs_last, low, 1024, qlow), low, 1024, wanted, center)
+                stage[0:192, qlow : qlow + 128] = grad_q
+                for h in range(3):
+                    lanes = slice(h * B + qlow, h * B + qlow + 128)
+                    probs_last[low:1024, lanes] = grad_scores[:, h * 128 : (h + 1) * 128]
+
+        poll_at("attend", i, 4)
+
+        @pl.when(s != 3)
+        def _():
             dk[0:TOP, :] += dot(probs[s], qz[s], NN)
 
         @pl.when(s == 3)
         def _():
             dk[...] += dot(probs_last[...], qz[s], NN)
 
-        dq[span, :] = (stage[0:192, 0:B] * HD**-0.5).T.astype(bf16)
+        a2[span, dq] = (stage[0:192, 0:B] * HD**-0.5).T.astype(bf16)
+        poll_at("after", i, 4)
         return carry
 
     dcz_t[...] = jnp.zeros(dcz_t.shape, bf16)
@@ -763,20 +755,20 @@
 
     stage_grad(6, dot(ctx_t[...], do_all[...], NN))
     poll("out")
-    dkb[...] = dk[...].astype(bf16)
-    dvb[...] = dv[...].astype(bf16)
-    for t, ref in enumerate((dq, dkb, dvb)):
-        stage_grad(7 + t, dot(ref[...], a1[...], TN))
+    a2[:, dkb] = dk[...].astype(bf16)
+    a2[:, dvb] = dv[...].astype(bf16)
+    for t, lanes in enumerate((dq, dkb, dvb)):
+        stage_grad(7 + t, dot(a2[:, lanes], a1[...], TN))
         poll(f"qkv{t}")
-    acc[9:10, 0:192] = column_sum(dq[...].astype(f32))
-    acc[9:10, 256:448] = column_sum(dvb[...].astype(f32))
+    acc[9:10, 0:192] = column_sum(a2[:, dq].astype(f32))
+    acc[9:10, 256:448] = column_sum(a2[:, dvb].astype(f32))
 
     def project_back(i, carry):
         s = me ^ (3 - i)
         span = rows(s)
-        grad = dot(dq[span, :], wqkv_ref[0], NN)
-        grad = grad + dot(dkb[span, :], wqkv_ref[1], NN)
-        grad = grad + dot(dvb[span, :], wqkv_ref[2], NN)
+        grad = dot(a2[span, dq], wqkv_ref[0], NN)
+        grad = grad + dot(a2[span, dkb], wqkv_ref[1], NN)
+        grad = grad + dot(a2[span, dvb], wqkv_ref[2], NN)
         hat, _ = layer_hat(xp[span, :].astype(f32))
         acc[0:1, :] += column_sum(grad * hat)
         acc[1:2, :] += column_sum(grad)
@@ -894,9 +886,8 @@
         shape(3, TOP, 768), shape(1024, 768), shape(4, 3, 8, B, dtype=f32),
         shape(192, 1024), shape(4, 4, 384, 128), shape(4, 192, 768), shape(1024, 768),
         shape(1024, 768), shape(1024, 768), shape(1024, 768), shape(1024, 768),
-        shape(192, 768), shape(768, 192), shape(3, 8, B, dtype=f32),
-        shape(1024, 192), shape(1024, 192, dtype=f32), shape(1024, 192, dtype=f32),
-        shape(1024, 192), shape(1024, 192), shape(B, 768, dtype=f32),
+        shape(192, 768), shape(768, 192), shape(8, 768, dtype=f32),
+        shape(1024, 192, dtype=f32), shape(1024, 192, dtype=f32), shape(B, 768, dtype=f32),
         shape(3, B, 768), shape(2, B, 768), shape(B, 768),
         shape(3, B, 768), shape(2, B, 768), shape(B, 768), shape(B, 768, dtype=f32),
         shape(8, 768, dtype=f32),

time: 119 us -> 116 us (0.975)
  Pallas kernels: 119 us -> 115 us
    pallas_call x1, Pallas kernels: 113 us -> 110 us  [per_device(): pl.pallas_call(layer_kernel, out_shape=[jax.ShapeDtypeStruct((B, 768), f3...]
where the time goes in v5:
time: 116 us
  Pallas kernels  115 us (99%)
    pallas_call x1, Pallas kernels, per_device(): pl.pallas_call(layer_kernel, out_shape=[jax.ShapeDtypeStruct((B, 768), f3...  110 us
    pallas_call x1, Pallas kernels, per_device(): pl.pallas_call(finish_kernel, out_shape=[out(share, 768), out(share, 768)...  5.51 us

profile of v5, /device:TPU:0, one launch (start us, length us, event | category | flops | bytes accessed | tf_op | source)
XLA Modules:
  0.0 115.9 jit_solution(13805896586725569740)
XLA Ops:
  0.7 109.6 %layer.1 = (f32[256,768]{1,0:T(8,128)}, f32[256,768]{1,0:T(8,128)}, f32[16,768]{1,0:T(8,128)}, bf16[3,2,4,64,384]{4,3,2,1,0:T(8,128)(2,1)}, bf16[3,2,4,64,384]{4...) custom-call(bf16[980,768]{1,0:T(8,128)(2,1)} %x_hbm.1, s32[980]{0:T(1024)} %ids_hbm.1, ...), custom_call_target="tpu_custom_call" | custom-call | tf_op jit(solution)/shard_map/layer/pallas_call | solution.py:903
  110.3 5.5 %finish.1 = (f32[245,768]{1,0:T(8,128)}, f32[245,768]{1,0:T(8,128)}, f32[768]{0:T(1024)}, f32[768]{0:T(1024)}, f32[3,192,768]{2,1,0:T(8,128)}, /*index=5*/f32[2,...) custom-call(f32[256,768]{1,0:T(8,128)} %get-tuple-element.35.block_h, ...), custom_call_target="tpu_custom_call" | custom-call | tf_op jit(solution)/shard_map/finish/pallas_call | solution.py:930

commit v6 on v5

--- a/solution.py
+++ b/solution.py
@@ -500,17 +500,15 @@
         gather_cot.copy(me, 1, across, pl.ds(q * 64, 64)).start()
     gather_wo.land_core()
     gather_wo.land_far()
-    for s in range(4):
-        gather_ctx(s).forward()
     loads[12].wait()
     loads[13].wait()
 
     zeros_w = jnp.zeros((HD, 768), bf16)
 
-    def middle(i, carry):
-        s = me ^ (3 - i)
+    def middle(s, carry):
         span = rows(s)
         ctx = gather_ctx(s)
+        ctx.forward()
         ctx.land_core()
         ctx.land_far()
         left = jnp.concatenate([ctx_all[j, s, 0:B, :] for j in range(4)], axis=1)
@@ -524,7 +522,7 @@
         )
         h = xp[span, :].astype(f32) + (branch + vec(2))
 
-        @pl.when(i == 3)
+        @pl.when(s == me)
         def _():
             block_ref[...] = h
 
@@ -804,10 +802,9 @@
     in_sem, out_sem,
 ):
     share = block_out.shape[0]
-    pairs = (
-        (down_hbm, down_v), (up_hbm, up_v), (qkv_hbm, qkv_v), (block_hbm, block_v), (input_hbm, input_v),
-        (out_hbm, out_v), (sums_hbm, sums),
-    )
+    pairs = [(down_hbm.at[p], down_v.at[p]) for p in range(3)] + [(up_hbm.at[p], up_v.at[p]) for p in range(3)]
+    pairs += [(qkv_hbm.at[p], qkv_v.at[p]) for p in range(3)]
+    pairs += [(block_hbm, block_v), (input_hbm, input_v), (out_hbm, out_v), (sums_hbm, sums)]
     loads = [pltpu.make_async_copy(src, dst, in_sem.at[k]) for k, (src, dst) in enumerate(pairs)]
     for load in loads:
         load.start()
@@ -824,34 +821,34 @@
                 put(slice(c * quarter, (c + 1) * quarter), slice(h * 384, (h + 1) * 384), source[p, h, c].astype(f32))
 
     for k, (source, wide, target) in enumerate(((down_v, down_w, grad_down), (up_v, up_w, grad_up))):
-        loads[k].wait()
         for p in range(3):
+            loads[3 * k + p].wait()
 
             def put(r, lanes, value):
                 wide[p * B + r.start : p * B + r.stop, lanes] = value
 
             widen(source, p, put)
-        save(wide, target)
-    loads[2].wait()
+            save(wide.at[p * B : (p + 1) * B], target.at[p * B : (p + 1) * B])
     for p in range(3):
+        loads[6 + p].wait()
 
         def put(r, lanes, value):
             qkv_w[p, r, lanes] = value
 
         widen(qkv_v, p, put)
-    save(qkv_w, grad_qkv)
-    for k, source, wide, target in ((3, block_v, block_w, block_out), (4, input_v, input_w, input_grad)):
+        save(qkv_w.at[p], grad_qkv.at[p])
+    for k, source, wide, target in ((9, block_v, block_w, block_out), (10, input_v, input_w, input_grad)):
         loads[k].wait()
         wide[...] = source[0:share, :]
         save(wide, target)
-    loads[5].wait()
+    loads[11].wait()
 
     def put(r, lanes, value):
         out_w[r, lanes] = value
 
     widen(out_v, 0, put)
     save(out_w, grad_out)
-    loads[6].wait()
+    loads[12].wait()
     for r, ref in enumerate((gain_first, shift_first, gain_second, shift_second, out_bias, down_bias)):
         ref[...] = sums[r, :]
     up_bias[...] = sums[8, :]
@@ -936,7 +933,7 @@
         in_specs=[anyspace] * 7,
         out_specs=[anyspace if k in (0, 1, 4, 6, 10, 12) else vmem for k in range(14)],
         scratch_shapes=[pltpu.VMEM(r.shape, r.dtype) for r in results]
-        + wide + [shape(192, 768, dtype=f32), shape(3, 192, 768, dtype=f32), dma((7,)), dma((6,))],
+        + wide + [shape(192, 768, dtype=f32), shape(3, 192, 768, dtype=f32), dma((13,)), dma((12,))],
         compiler_params=pltpu.CompilerParams(vmem_limit_bytes=60 * 2**20),
         name="finish",
     )(*results)

time: 116 us -> 116 us (level)
  no operation moved by 1% of the time
where the time goes in v6:
time: 116 us
  Pallas kernels  115 us (99%)
    pallas_call x1, Pallas kernels, per_device(): pl.pallas_call(layer_kernel, out_shape=[jax.ShapeDtypeStruct((B, 768), f3...  110 us
    pallas_call x1, Pallas kernels, per_device(): pl.pallas_call(finish_kernel, out_shape=[out(share, 768), out(share, 768)...  5.29 us

profile of v6, /device:TPU:0, one launch (start us, length us, event | category | flops | bytes accessed | tf_op | source)
XLA Modules:
  0.0 115.7 jit_solution(9908464864408251611)
XLA Ops:
  0.7 109.6 %layer.1 = (f32[256,768]{1,0:T(8,128)}, f32[256,768]{1,0:T(8,128)}, f32[16,768]{1,0:T(8,128)}, bf16[3,2,4,64,384]{4,3,2,1,0:T(8,128)(2,1)}, bf16[3,2,4,64,384]{4...) custom-call(bf16[980,768]{1,0:T(8,128)(2,1)} %x_hbm.1, s32[980]{0:T(1024)} %ids_hbm.1, ...), custom_call_target="tpu_custom_call" | custom-call | tf_op jit(solution)/shard_map/layer/pallas_call | solution.py:900
  110.3 5.3 %finish.1 = (f32[245,768]{1,0:T(8,128)}, f32[245,768]{1,0:T(8,128)}, f32[768]{0:T(1024)}, f32[768]{0:T(1024)}, f32[3,192,768]{2,1,0:T(8,128)}, /*index=5*/f32[2,...) custom-call(f32[256,768]{1,0:T(8,128)} %get-tuple-element.35.block_h, ...), custom_call_target="tpu_custom_call" | custom-call | tf_op jit(solution)/shard_map/finish/pallas_call | solution.py:927
